TPU v7x, 32 devices: a whole 2x2x4 slice. The times are simulated.
32 devices in a mesh: row: 4 (over y, core), col: 8 (over z, x).
Axes of the slice: x: 2, y: 2, z: 4, core: 2. Of those that a mesh axis runs over, the one named last changes fastest.
Arguments:
- parent_front: float32 [4, 4, 256, 2, 8, 256], P(None, 'row', None, None, 'col'), may hold values from -6 to 48, as said below
- child_tiles: bfloat16 [32, 16, 256, 256], P(('row', 'col')), may hold values from -6 to 6
- tile_target: int32 [32, 16, 2], replicated, may hold values from 0 to 15, as said below
Outputs:
- factored_front: float32 [4, 4, 256, 2, 8, 256], P(None, 'row', None, None, 'col')
Inputs may be any that keep to these rules, and one draw needn't show every extreme that they name: The leading 6 * 256 rows and columns of parent_front form a symmetric matrix with diagonal entries in 32 to 48 and other entries of magnitude at most 30 / 1536. tile_target[d, s] is the parent tile (row, column) into which tile s of device d is added (device d is mesh row d // 8, column d % 8); rows are 6 or more. Parent tile (I, J) lives on mesh row I % 4, column J % 8. The 16 tiles of one device go to 16 different devices, and one device receives a tile from every device.
All inputs are finite; a program needn't handle non-finite values.
Results may differ from a plain program's by a relative error of at most 0.0003.
Values may be sent and summed in bfloat16 or wider, within the bound.
A program may use at most 192 MiB of HBM per device.

v0:
```python
import jax
import jax.numpy as jnp
from jax import lax
from jax.sharding import PartitionSpec as P

PANELS = 6


def broadcast(shard, axis, root):
    mine = lax.axis_index(axis) == root
    return lax.psum(jnp.where(mine, shard, jnp.zeros_like(shard)), axis)


def shards(parent_front, child_tiles, tile_target):
    lrows = parent_front.shape[0]
    tile = parent_front.shape[2]
    lcols = parent_front.shape[3]
    row_count = lax.axis_size("row")
    col_count = lax.axis_size("col")
    devices = row_count * col_count
    my_row = lax.axis_index("row")
    my_col = lax.axis_index("col")
    myself = my_row * col_count + my_col
    front = parent_front.reshape(lrows, tile, lcols, tile)
    stored = child_tiles.shape[1]
    held = child_tiles.reshape(stored, tile, tile)
    rows_all = tile_target[:, :, 0]
    cols_all = tile_target[:, :, 1]
    owner_all = rows_all % row_count * col_count + cols_all % col_count
    local_all = rows_all // row_count * lcols + cols_all // col_count
    peers = jnp.arange(devices, dtype=jnp.int32)
    my_owner = lax.dynamic_index_in_dim(owner_all, myself, 0, keepdims=False)
    sending = my_owner[None, :] == peers[:, None]
    present = jnp.any(sending, axis=1)
    picked = jnp.sum(jnp.where(sending, jnp.arange(stored, dtype=jnp.int32)[None, :], 0), axis=1)
    outgoing = jnp.where(present[:, None, None], held[picked], jnp.zeros((), jnp.bfloat16))
    arrived = lax.all_to_all(outgoing, ("row", "col"), split_axis=0, concat_axis=0, tiled=True)
    landing = owner_all == myself
    came = jnp.any(landing, axis=1)
    where_to = jnp.sum(jnp.where(landing, local_all, 0), axis=1)
    slots = jnp.arange(lrows * lcols, dtype=jnp.int32)
    onehot = ((where_to[:, None] == slots[None, :]) & came[:, None]).astype(jnp.bfloat16)
    onehot = onehot.reshape(devices, lrows, lcols)
    summed = jnp.einsum("dij,dxy->ixjy", onehot, arrived, preferred_element_type=jnp.float32)
    front = front + summed
    row_ids = my_row + row_count * jnp.arange(lrows, dtype=jnp.int32)
    col_ids = my_col + col_count * jnp.arange(lcols, dtype=jnp.int32)
    stride = col_count // row_count
    pick_rows = my_col // row_count + stride * jnp.arange(lcols, dtype=jnp.int32)
    for step in range(PANELS):
        pivot = broadcast(
            front[step // row_count, :, step // col_count, :], "row", step % row_count
        )
        lower = jnp.linalg.cholesky(pivot)
        column = front[:, :, step // col_count, :].reshape(lrows * tile, tile)
        solved = jax.scipy.linalg.solve_triangular(lower, column.T, lower=True).T.reshape(
            lrows, tile, tile
        )
        factor = jnp.where((row_ids == step)[:, None, None], lower[None, :, :], solved)
        factor = jnp.where((row_ids >= step)[:, None, None], factor, jnp.zeros((), jnp.float32))
        row_panel = broadcast(factor, "col", step % col_count)
        chosen = row_panel[pick_rows]
        col_panel = broadcast(chosen, "row", my_col % row_count)
        update = jnp.einsum("iak,jbk->iajb", row_panel, col_panel, precision=lax.Precision.HIGHEST)
        trailing = front - update
        upper_zero = (row_ids[:, None] == step) & (col_ids[None, :] > step)
        trailing = jnp.where(upper_zero[:, None, :, None], jnp.zeros((), jnp.float32), trailing)
        front = jnp.where(
            (col_ids == step)[None, None, :, None], row_panel[:, :, None, :], trailing
        )
    return front.reshape(parent_front.shape)


def solution(mesh):
    return jax.shard_map(
        shards,
        mesh=mesh,
        in_specs=(
            P(None, "row", None, None, "col", None),
            P(("row", "col"), None, None, None),
            P(),
        ),
        out_specs=P(None, "row", None, None, "col", None),
        check_vma=False,
    )
```

profile of v0, /device:TPU:0, one launch (start us, length us, event | category | flops | bytes accessed | tf_op | source)
XLA Modules:
  0.0 1461.0 jit_solution(10553494222959239131)
XLA Ops:
  8.2 2.8 gather_fusion
  10.9 4.5 broadcast_select_fusion
  15.4 7.4 all-to-all-start
  22.9 4.0 copy.67
  27.0 91.0 %all-to-all-done = bf16[32,256,256]{2,1,0:T(8,128)(2,1)} async-done(((bf16[32,256,256]{2,1,0:T(8,128)(2,1)}), bf16[32,256,256]{2,1,0:T(8,128)(2,1)}, u32[]{:S(2)}, u32[]{:S(2)}) %all-to-all-start) | async-done | bytes 4194336 | tf_op jit(solution)/shard_map/all_to_all | solution.py:37
  118.0 4.7 fusion
  131.8 25.9 %all-reduce.20.cloned.1.call-done = f32[256,256]{0,1:T(8,128)} async-done(((f32[256,256]{0,1:T(8,128)}), f32[256,256]{0,1:T(8,128)}) %all-reduce.20.cloned.1.call-update) | async-done | bytes 262160 | tf_op jit(solution)/shard_map/psum | solution.py:11
  160.5 11.7 cholesky.298
  172.3 9.8 custom-call.21
  184.3 11.7 cholesky.315
  200.4 4.1 while.12
  205.2 20.5 %custom-call.22 = f32[2,128,128]{1,2,0:T(8,128)S(1)} custom-call(f32[2,128,128]{2,1,0:T(8,128)} %copy-done.20), custom_call_target="InvertDiagBlocksLowerTriangular" | custom-call | tf_op jit(solution)/shard_map/jit(_solve_triangular)/triangular_solve | solution.py:56
  231.4 77.1 %all-reduce.22.cloned.1.call-done = f32[4,256,256]{2,1,0:T(8,128)} async-done(((f32[4,256,256]{2,1,0:T(8,128)}), f32[4,256,256]{2,1,0:T(8,128)}) %all-reduce.22.cloned.1.call-update) | async-done | bytes 1048592 | tf_op jit(solution)/shard_map/psum | solution.py:11
  308.5 2.7 gather_fusion.1
  314.5 30.8 %all-reduce.24.cloned.1.call-done = f32[2,256,256]{2,1,0:T(8,128)} async-done(((f32[2,256,256]{2,1,0:T(8,128)}), f32[2,256,256]{2,1,0:T(8,128)}) %all-reduce.24.cloned.1.call-update) | async-done | bytes 524304 | tf_op jit(solution)/shard_map/psum | solution.py:11
  345.3 3.4 select_select_fusion.4
  354.9 28.0 %all-reduce.26.cloned.1.call-done = f32[256,256]{0,1:T(8,128)} async-done(((f32[256,256]{0,1:T(8,128)}), f32[256,256]{0,1:T(8,128)}) %all-reduce.26.cloned.1.call-update) | async-done | bytes 262160 | tf_op jit(solution)/shard_map/psum | solution.py:11
  385.0 11.7 cholesky.332
  396.8 9.8 custom-call.23
  407.1 11.7 cholesky.349
  421.5 4.3 while.13
  425.9 19.7 %custom-call.24 = f32[2,128,128]{1,2,0:T(8,128)S(1)} custom-call(f32[2,128,128]{2,1,0:T(8,128)S(1)} %get-tuple-element.46), custom_call_target="InvertDiagBlocksLowerTriangular" | custom-call | tf_op jit(solution)/shard_map/jit(_solve_triangular)/triangular_solve | solution.py:56
  449.1 78.0 %all-reduce.28.cloned.1.call-done = f32[4,256,256]{2,1,0:T(8,128)} async-done(((f32[4,256,256]{2,1,0:T(8,128)}), f32[4,256,256]{2,1,0:T(8,128)}) %all-reduce.28.cloned.1.call-update) | async-done | bytes 1048592 | tf_op jit(solution)/shard_map/psum | solution.py:11
  531.4 31.4 %all-reduce.30.cloned.1.call-done = f32[2,256,256]{2,1,0:T(8,128)} async-done(((f32[2,256,256]{2,1,0:T(8,128)}), f32[2,256,256]{2,1,0:T(8,128)}) %all-reduce.30.cloned.1.call-update) | async-done | bytes 524304 | tf_op jit(solution)/shard_map/psum | solution.py:11
  562.9 4.0 select_select_fusion.3
  571.1 28.6 %all-reduce.32.cloned.1.call-done = f32[256,256]{0,1:T(8,128)} async-done(((f32[256,256]{0,1:T(8,128)}), f32[256,256]{0,1:T(8,128)}) %all-reduce.32.cloned.1.call-update) | async-done | bytes 262160 | tf_op jit(solution)/shard_map/psum | solution.py:11
  602.5 11.7 cholesky.366
  614.3 9.8 custom-call.25
  626.3 11.7 cholesky.383
  641.4 5.5 while.14
  647.5 20.5 %custom-call.26 = f32[2,128,128]{1,2,0:T(8,128)S(1)} custom-call(f32[2,128,128]{2,1,0:T(8,128)} %copy-done.21), custom_call_target="InvertDiagBlocksLowerTriangular" | custom-call | tf_op jit(solution)/shard_map/jit(_solve_triangular)/triangular_solve | solution.py:56
  673.8 78.1 %all-reduce.34.cloned.1.call-done = f32[4,256,256]{2,1,0:T(8,128)} async-done(((f32[4,256,256]{2,1,0:T(8,128)}), f32[4,256,256]{2,1,0:T(8,128)}) %all-reduce.34.cloned.1.call-update) | async-done | bytes 1048592 | tf_op jit(solution)/shard_map/psum | solution.py:11
  751.9 2.7 gather_fusion.3
  757.9 30.8 %all-reduce.36.cloned.1.call-done = f32[2,256,256]{2,1,0:T(8,128)} async-done(((f32[2,256,256]{2,1,0:T(8,128)}), f32[2,256,256]{2,1,0:T(8,128)}) %all-reduce.36.cloned.1.call-update) | async-done | bytes 524304 | tf_op jit(solution)/shard_map/psum | solution.py:11
  788.7 3.4 select_select_fusion.2
  796.1 30.2 %all-reduce.38.cloned.1.call-done = f32[256,256]{0,1:T(8,128)} async-done(((f32[256,256]{0,1:T(8,128)}), f32[256,256]{0,1:T(8,128)}) %all-reduce.38.cloned.1.call-update) | async-done | bytes 262160 | tf_op jit(solution)/shard_map/psum | solution.py:11
  828.4 11.7 cholesky.400
  840.2 9.8 custom-call.27
  850.5 11.7 cholesky.417
  864.9 4.3 while.15
  869.2 19.7 %custom-call.28 = f32[2,128,128]{1,2,0:T(8,128)S(1)} custom-call(f32[2,128,128]{2,1,0:T(8,128)S(1)} %get-tuple-element.48), custom_call_target="InvertDiagBlocksLowerTriangular" | custom-call | tf_op jit(solution)/shard_map/jit(_solve_triangular)/triangular_solve | solution.py:56
  892.5 78.1 %all-reduce.40.cloned.1.call-done = f32[4,256,256]{2,1,0:T(8,128)} async-done(((f32[4,256,256]{2,1,0:T(8,128)}), f32[4,256,256]{2,1,0:T(8,128)}) %all-reduce.40.cloned.1.call-update) | async-done | bytes 1048592 | tf_op jit(solution)/shard_map/psum | solution.py:11
  970.6 2.7 gather_fusion.4
  976.9 30.8 %all-reduce.42.cloned.1.call-done = f32[2,256,256]{2,1,0:T(8,128)} async-done(((f32[2,256,256]{2,1,0:T(8,128)}), f32[2,256,256]{2,1,0:T(8,128)}) %all-reduce.42.cloned.1.call-update) | async-done | bytes 524304 | tf_op jit(solution)/shard_map/psum | solution.py:11
  1007.6 3.4 select_select_fusion.1
  1017.2 28.0 %all-reduce.44.cloned.1.call-done = f32[256,256]{0,1:T(8,128)} async-done(((f32[256,256]{0,1:T(8,128)}), f32[256,256]{0,1:T(8,128)}) %all-reduce.44.cloned.1.call-update) | async-done | bytes 262160 | tf_op jit(solution)/shard_map/psum | solution.py:11
  1047.3 11.7 cholesky.434
  1059.1 9.8 custom-call.29
  1069.4 11.7 cholesky.451
  1083.8 4.2 while.16
  1088.0 19.7 %custom-call.30 = f32[2,128,128]{1,2,0:T(8,128)S(1)} custom-call(f32[2,128,128]{2,1,0:T(8,128)S(1)} %get-tuple-element.49), custom_call_target="InvertDiagBlocksLowerTriangular" | custom-call | tf_op jit(solution)/shard_map/jit(_solve_triangular)/triangular_solve | solution.py:56
  1111.3 78.2 %all-reduce.46.cloned.1.call-done = f32[4,256,256]{2,1,0:T(8,128)} async-done(((f32[4,256,256]{2,1,0:T(8,128)}), f32[4,256,256]{2,1,0:T(8,128)}) %all-reduce.46.cloned.1.call-update) | async-done | bytes 1048592 | tf_op jit(solution)/shard_map/psum | solution.py:11
  1193.8 31.4 %all-reduce.48.cloned.1.call-done = f32[2,256,256]{2,1,0:T(8,128)} async-done(((f32[2,256,256]{2,1,0:T(8,128)}), f32[2,256,256]{2,1,0:T(8,128)}) %all-reduce.48.cloned.1.call-update) | async-done | bytes 524304 | tf_op jit(solution)/shard_map/psum | solution.py:11
  1225.3 4.0 select_select_fusion
  1233.3 28.9 %all-reduce.50.cloned.1.call-done = f32[256,256]{0,1:T(8,128)} async-done(((f32[256,256]{0,1:T(8,128)}), f32[256,256]{0,1:T(8,128)}) %all-reduce.50.cloned.1.call-update) | async-done | bytes 262160 | tf_op jit(solution)/shard_map/psum | solution.py:11
  1264.3 11.7 cholesky.468
  1276.1 9.8 custom-call.31
  1286.4 11.7 cholesky.485
  1300.8 4.3 while.17
  1305.1 19.7 %custom-call.32 = f32[2,128,128]{1,2,0:T(8,128)S(1)} custom-call(f32[2,128,128]{2,1,0:T(8,128)S(1)} %get-tuple-element.50), custom_call_target="InvertDiagBlocksLowerTriangular" | custom-call | tf_op jit(solution)/shard_map/jit(_solve_triangular)/triangular_solve | solution.py:56
  1328.4 78.2 %all-reduce.52.cloned.1.call-done = f32[4,256,256]{2,1,0:T(8,128)} async-done(((f32[4,256,256]{2,1,0:T(8,128)}), f32[4,256,256]{2,1,0:T(8,128)}) %all-reduce.52.cloned.1.call-update) | async-done | bytes 1048592 | tf_op jit(solution)/shard_map/psum | solution.py:11
  1410.8 31.5 %all-reduce.54.cloned.1.call-done = f32[2,256,256]{2,1,0:T(8,128)} async-done(((f32[2,256,256]{2,1,0:T(8,128)}), f32[2,256,256]{2,1,0:T(8,128)}) %all-reduce.54.cloned.1.call-update) | async-done | bytes 524304 | tf_op jit(solution)/shard_map/psum | solution.py:11
  1442.3 5.5 select_bitcast_fusion
  1447.8 6.0 copy.107
  (305 shorter events, 141.3 us)
Async XLA Ops:
  6.5 1.6 copy-start
  15.4 7.5 copy-start.13
  15.4 102.6 %all-to-all-start = ((bf16[32,256,256]{2,1,0:T(8,128)(2,1)}), bf16[32,256,256]{2,1,0:T(8,128)(2,1)}, u32[]{:S(2)}, u32[]{:S(2)}) async-start(bf16[32,256,256]{2,1,0:T(8,128)(2,1)} %broadcast_select_fusion), calls=%async_computation | async-start | bytes 8388608 | tf_op jit(solution)/shard_map/all_to_all | solution.py:37
  22.9 134.9 %all-reduce.20.cloned.1.call-start = ((), (), s32[]{:S(2)}) async-start(), calls=%async_computation.1 | async-start | bytes 524288 | tf_op jit(solution)/shard_map/psum | solution.py:11
  127.8 180.7 %all-reduce.22.cloned.1.call-start = ((), (), s32[]{:S(2)}) async-start(), calls=%async_computation.2 | async-start | bytes 2097152 | tf_op jit(solution)/shard_map/psum | solution.py:11
  159.8 0.7 copy-start.18
  196.0 2.0 copy-start.16
  204.5 0.7 copy-start.20
  227.5 2.6 copy-start.14
  231.3 114.0 %all-reduce.24.cloned.1.call-start = ((), (), s32[]{:S(2)}) async-start(), calls=%async_computation.3 | async-start | bytes 1048576 | tf_op jit(solution)/shard_map/psum | solution.py:11
  308.5 4.7 copy-start.7
  313.1 69.9 %all-reduce.26.cloned.1.call-start = ((), (), s32[]{:S(2)}) async-start(), calls=%async_computation.4 | async-start | bytes 524288 | tf_op jit(solution)/shard_map/psum | solution.py:11
  348.7 1.3 copy-start.3
  350.8 1.2 slice-start
  350.8 176.4 %all-reduce.28.cloned.1.call-start = ((), (), s32[]{:S(2)}) async-start(), calls=%async_computation.5 | async-start | bytes 2097152 | tf_op jit(solution)/shard_map/psum | solution.py:11
  425.8 21.7 %copy-start.22 = (s32[2,2]{1,0:T(2,128)}, s32[2,2]{1,0:T(2,128)S(1)}, u32[]{:S(2)}) copy-start(s32[2,2]{1,0:T(2,128)S(1)} %get-tuple-element.529) | copy-start | bytes 52
  449.1 113.8 %all-reduce.30.cloned.1.call-start = ((), (), s32[]{:S(2)}) async-start(), calls=%async_computation.6 | async-start | bytes 1048576 | tf_op jit(solution)/shard_map/psum | solution.py:11
  527.2 2.9 copy-start.8
  530.0 69.8 %all-reduce.32.cloned.1.call-start = ((), (), s32[]{:S(2)}) async-start(), calls=%async_computation.7 | async-start | bytes 524288 | tf_op jit(solution)/shard_map/psum | solution.py:11
  567.6 184.3 %all-reduce.34.cloned.1.call-start = ((), (), s32[]{:S(2)}) async-start(), calls=%async_computation.8 | async-start | bytes 2097152 | tf_op jit(solution)/shard_map/psum | solution.py:11
  601.8 0.7 copy-start.19
  638.0 2.6 copy-start.17
  646.9 0.7 copy-start.21
  669.9 2.6 copy-start.15
  673.7 115.0 %all-reduce.36.cloned.1.call-start = ((), (), s32[]{:S(2)}) async-start(), calls=%async_computation.9 | async-start | bytes 1048576 | tf_op jit(solution)/shard_map/psum | solution.py:11
  751.9 4.7 copy-start.9
  756.5 69.8 %all-reduce.38.cloned.1.call-start = ((), (), s32[]{:S(2)}) async-start(), calls=%async_computation.10 | async-start | bytes 524288 | tf_op jit(solution)/shard_map/psum | solution.py:11
  792.1 1.3 copy-start.4
  794.2 1.2 slice-start.1
  794.2 176.4 %all-reduce.40.cloned.1.call-start = ((), (), s32[]{:S(2)}) async-start(), calls=%async_computation.11 | async-start | bytes 2097152 | tf_op jit(solution)/shard_map/psum | solution.py:11
  796.1 68.8 %copy-start.23 = (s32[2,2]{1,0:T(2,128)S(1)}, s32[2,2]{1,0:T(2,128)}, u32[]{:S(2)}) copy-start(s32[2,2]{1,0:T(2,128)} %get-tuple-element.530) | copy-start | bytes 52
  892.5 115.2 %all-reduce.42.cloned.1.call-start = ((), (), s32[]{:S(2)}) async-start(), calls=%async_computation.12 | async-start | bytes 1048576 | tf_op jit(solution)/shard_map/psum | solution.py:11
  970.6 4.9 copy-start.11
  973.3 34.3 %copy-start.5 = (f32[4,256,2,256]{1,3,2,0:T(8,128)S(1)}, f32[4,256,2,256]{1,3,2,0:T(8,128)}, u32[]{:S(2)}) copy-start(f32[4,256,2,256]{1,3,2,0:T(8,128)} %copy-done.4) | copy-start | bytes 6291460
  975.4 69.8 %all-reduce.44.cloned.1.call-start = ((), (), s32[]{:S(2)}) async-start(), calls=%async_computation.13 | async-start | bytes 524288 | tf_op jit(solution)/shard_map/psum | solution.py:11
  1011.0 1.3 copy-start.6
  1013.1 1.2 slice-start.2
  1013.1 176.5 %all-reduce.46.cloned.1.call-start = ((), (), s32[]{:S(2)}) async-start(), calls=%async_computation.14 | async-start | bytes 2097152 | tf_op jit(solution)/shard_map/psum | solution.py:11
  1111.3 114.0 %all-reduce.48.cloned.1.call-start = ((), (), s32[]{:S(2)}) async-start(), calls=%async_computation.15 | async-start | bytes 1048576 | tf_op jit(solution)/shard_map/psum | solution.py:11
  1189.6 2.9 copy-start.12
  1192.4 69.9 %all-reduce.50.cloned.1.call-start = ((), (), s32[]{:S(2)}) async-start(), calls=%async_computation.16 | async-start | bytes 524288 | tf_op jit(solution)/shard_map/psum | solution.py:11
  1229.3 3.7 copy-start.2
  1230.1 176.5 %all-reduce.52.cloned.1.call-start = ((), (), s32[]{:S(2)}) async-start(), calls=%async_computation.17 | async-start | bytes 2097152 | tf_op jit(solution)/shard_map/psum | solution.py:11
  1328.4 114.0 %all-reduce.54.cloned.1.call-start = ((), (), s32[]{:S(2)}) async-start(), calls=%async_computation.18 | async-start | bytes 1048576 | tf_op jit(solution)/shard_map/psum | solution.py:11
  1406.6 2.9 copy-start.10
  1442.3 11.5 copy-start.1
Sparse Core Ops, SparseCore 0:
  127.9 29.7 all-reduce.19
  231.4 76.9 all-reduce.21
  313.2 32.0 all-reduce.23
  350.9 31.9 all-reduce.25
  449.2 77.9 all-reduce.27
  530.1 32.7 all-reduce.29
  567.7 31.9 all-reduce.31
  673.8 77.9 all-reduce.33
  756.6 32.0 all-reduce.35
  794.3 31.9 all-reduce.37
  892.6 77.9 all-reduce.39
  975.5 32.0 all-reduce.41
  1013.2 31.9 all-reduce.43
  1111.4 78.1 all-reduce.45
  1192.5 32.7 all-reduce.47
  1230.2 31.9 all-reduce.49
  1328.5 78.1 all-reduce.51
  1409.5 32.7 all-reduce.53
where the time goes:
time: 1470 us; the launch traced here: 1460 us
  waiting for transfers between devices  916 us (62%)
  other arithmetic  366 us (25%)
  local copies, waits for them, and re-layouts  99.2 us (7%)
  matrix products  45.5 us (3%)
  between operations  22.6 us (2%)
    psum x18, waiting for transfers between devices, broadcast(): return lax.psum(jnp.where(mine, shard, jnp.zeros_like(shard)), axis)  824 us
    another operation x41, other arithmetic, shards(): lower = jnp.linalg.cholesky(pivot)  207 us
    another operation x13, other arithmetic, shards(): jax.scipy.linalg.solve_triangular(lower, column.T, lower=True)  123 us
    all_to_all x1, waiting for transfers between devices, shards(): lax.all_to_all(outgoing, ('row', 'col'), split_axis=0, concat_axis=0, til...  91 us
  transfers between devices with their start and end apart: 19, of which 19 were waited for; matrix products, arithmetic and copies ran while one was open for 2% of the time, Pallas kernels for 0%

commit v1 on v0

v1 whole, which is shorter than its diff:
```python
import jax
import jax.numpy as jnp
from jax import lax
from jax.sharding import PartitionSpec as P

PANELS = 6
HIGH = lax.Precision.HIGH


def dot(a, b):
    return jnp.dot(a, b, precision=HIGH)


def dot_t(a, b):
    return lax.dot_general(a, b, (((1,), (1,)), ((), ())), precision=HIGH)


def lower_inverse(lower):
    size = lower.shape[0]
    eye = jnp.eye(size, dtype=jnp.float32)
    inv_diag = 1.0 / jnp.sum(lower * eye, axis=0)
    power = eye - lower * inv_diag[None, :]
    result = eye + power
    reach = 2
    while reach < size:
        power = dot(power, power)
        result = result + dot(result, power)
        reach *= 2
    return result * inv_diag[:, None]


def leading_factor(first, row_count, col_count, my_row, my_col):
    tile = first.shape[1]
    grid = lax.all_gather(first[0], ("row", "col"), axis=0)
    grid = grid.reshape(row_count, col_count, tile, tile)
    pairs = [(i, j) for j in range(row_count, PANELS) for i in range(j, PANELS)]
    extra = {}
    if pairs:
        mine = [
            jnp.where(
                (my_row == i % row_count) & (my_col == j),
                first[i // row_count],
                jnp.zeros((), jnp.float32),
            )
            for i, j in pairs
        ]
        summed = lax.psum(jnp.stack(mine), ("row", "col"))
        extra = {pair: summed[n] for n, pair in enumerate(pairs)}

    def tile_at(i, j):
        if i < row_count:
            return grid[i, j]
        if j < row_count:
            return grid[j, i].T
        return extra[i, j]

    lead = {}
    inverses = []
    below = None
    for k in range(PANELS):
        column = jnp.concatenate([tile_at(i, k) for i in range(k, PANELS)], axis=0)
        if k:
            left = jnp.concatenate(
                [jnp.concatenate([lead[i, j] for j in range(k)], axis=1) for i in range(k, PANELS)], axis=0
            )
            column = column - dot_t(left, left[:tile])
        pivot = column[:tile]
        lower = jnp.linalg.cholesky(pivot)
        inverse = lower_inverse(lower)
        inverses.append(inverse)
        lead[k, k] = lower
        if k + 1 < PANELS:
            below = dot_t(column[tile:], inverse)
            for i in range(k + 1, PANELS):
                lead[i, k] = below[(i - k - 1) * tile:(i - k) * tile]
    return lead, inverses


def shards(parent_front, child_tiles, tile_target):
    lrows = parent_front.shape[0]
    tile = parent_front.shape[2]
    lcols = parent_front.shape[3]
    row_count = lax.axis_size("row")
    col_count = lax.axis_size("col")
    devices = row_count * col_count
    my_row = lax.axis_index("row")
    my_col = lax.axis_index("col")
    myself = my_row * col_count + my_col
    front = parent_front.reshape(lrows, tile, lcols, tile)
    first = PANELS // row_count
    lead_rows = -(-PANELS // row_count)

    lead, inverses = leading_factor(front[:lead_rows, :, 0, :], row_count, col_count, my_row, my_col)

    stored = child_tiles.shape[1]
    held = child_tiles.reshape(stored, tile, tile)
    rows_all = tile_target[:, :, 0]
    cols_all = tile_target[:, :, 1]
    owner_all = rows_all % row_count * col_count + cols_all % col_count
    local_all = rows_all // row_count * lcols + cols_all // col_count
    peers = jnp.arange(devices, dtype=jnp.int32)
    my_owner = lax.dynamic_index_in_dim(owner_all, myself, 0, keepdims=False)
    sending = my_owner[None, :] == peers[:, None]
    present = jnp.any(sending, axis=1)
    picked = jnp.sum(jnp.where(sending, jnp.arange(stored, dtype=jnp.int32)[None, :], 0), axis=1)
    outgoing = jnp.where(present[:, None, None], held[picked], jnp.zeros((), jnp.bfloat16))
    arrived = lax.all_to_all(outgoing, ("row", "col"), split_axis=0, concat_axis=0, tiled=True)
    landing = owner_all == myself
    came = jnp.any(landing, axis=1)
    where_to = jnp.sum(jnp.where(landing, local_all, 0), axis=1)
    slots = jnp.arange(lrows * lcols, dtype=jnp.int32)
    onehot = ((where_to[:, None] == slots[None, :]) & came[:, None]).astype(jnp.bfloat16)
    onehot = onehot.reshape(devices, lrows, lcols)[:, first:]
    summed = jnp.einsum("dij,dxy->ijxy", onehot, arrived, preferred_element_type=jnp.float32)
    lower_front = front[first:].transpose(0, 2, 1, 3) + summed
    count = lrows - first

    panel = lax.all_gather(lower_front[:, 0], "col", axis=0)[:PANELS]
    pick = my_col // row_count + col_count // row_count * jnp.arange(lcols, dtype=jnp.int32) - first
    chosen = panel[:, jnp.clip(pick, 0, count - 1)]
    root = my_row == my_col % row_count
    chosen = lax.psum(jnp.where(root, chosen, jnp.zeros((), jnp.float32)), "row")
    stack = jnp.concatenate([panel, chosen], axis=1).reshape(PANELS, (count + lcols) * tile, tile)
    solved = []
    for k in range(PANELS):
        value = stack[k]
        if k:
            row = jnp.concatenate([lead[k, j] for j in range(k)], axis=1)
            value = value - dot_t(jnp.concatenate(solved, axis=1), row)
        solved.append(dot_t(value, inverses[k]))
    wide = jnp.concatenate(solved, axis=1)
    update = dot_t(wide[:count * tile], wide[count * tile:])
    update = update.reshape(count, tile, lcols, tile)
    row_ids = my_row + row_count * jnp.arange(lrows, dtype=jnp.int32)
    col_ids = my_col + col_count * jnp.arange(lcols, dtype=jnp.int32)
    trailing = lower_front.transpose(0, 2, 1, 3) - update
    at = jnp.minimum(my_col, PANELS - 1)
    mine = lax.dynamic_index_in_dim(
        wide[:count * tile].reshape(count, tile, PANELS, tile), at, 2, keepdims=True
    )
    in_panel = (col_ids < PANELS)[None, None, :, None]
    below = jnp.where(in_panel, mine, trailing)
    zero = jnp.zeros((tile, tile), jnp.float32)
    grid = jnp.stack([jnp.stack([lead.get((i, j), zero) for j in range(PANELS)]) for i in range(PANELS)])
    tops = []
    for i in range(lead_rows):
        picked_tile = grid[jnp.minimum(my_row + row_count * i, PANELS - 1), at]
        tops.append(jnp.where((col_ids < PANELS)[None, :, None], picked_tile[:, None, :], 0.0))
    out = []
    for i in range(lrows):
        if i < first:
            out.append(tops[i])
        elif i < lead_rows:
            out.append(jnp.where(row_ids[i] < PANELS, tops[i], below[i - first]))
        else:
            out.append(below[i - first])
    return jnp.stack(out).reshape(parent_front.shape)


def solution(mesh):
    return jax.shard_map(
        shards,
        mesh=mesh,
        in_specs=(
            P(None, "row", None, None, "col", None),
            P(("row", "col"), None, None, None),
            P(),
        ),
        out_specs=P(None, "row", None, None, "col", None),
        check_vma=False,
    )
```

time: 1470 us -> 758 us (0.52)
  waiting for transfers between devices: 916 us -> 278 us
  other arithmetic: 366 us -> 243 us
  matrix products: 45.5 us -> 86.4 us
    psum x18 -> x2, waiting for transfers between devices: 824 us -> 208 us  [the longest x1 145 us: leading_factor(): summed = lax.psum(jnp.stack(mine), ('row', 'col'))]
    another operation x54 -> x46, other arithmetic: 330 us -> 213 us  [the longest x42 211 us: leading_factor(): lower = jnp.linalg.cholesky(pivot)]
    all_to_all x1, waiting for transfers between devices: 91 us -> 0.01 us  [shards(): lax.all_to_all(outgoing, ('row', 'col'), split_axis=0, concat_axis=0, til...]
    all_gather x0 -> x2, waiting for transfers between devices: none -> 70.4 us  [the longest x1 70.4 us: leading_factor(): grid = lax.all_gather(first[0], ('row', 'col'), axis=0)]
    dot_general x7 -> x107, matrix products: 28.3 us -> 76.5 us  [the longest x22 37.8 us: dot_t(): return lax.dot_general(a, b, (((1,), (1,)), ((), ())), precision=HIGH)]
    unnamed x49 -> x222, local copies, waits for them, and re-layouts: 11 us -> 46.6 us
    another operation x61 -> x21, local copies, waits for them, and re-layouts: 33 us -> 3.95 us  [the longest x14 2.46 us: leading_factor(): lower = jnp.linalg.cholesky(pivot)]
  transfers between devices with their start and end apart: 19 -> 5, of which waited for: 19 -> 3; matrix products, arithmetic and copies ran while one was open for 2% -> 46% of each run, Pallas kernels for 0% -> 0%
where the time goes in v1:
time: 758 us; the launch traced here: 750 us
  waiting for transfers between devices  278 us (37%)
  other arithmetic  243 us (32%)
  local copies, waits for them, and re-layouts  110 us (15%)
  matrix products  86.4 us (11%)
  between operations  24.1 us (3%)
  starting transfers between devices  7.76 us (1%)
    another operation x42, other arithmetic, leading_factor(): lower = jnp.linalg.cholesky(pivot)  211 us
    psum x1, waiting for transfers between devices, leading_factor(): summed = lax.psum(jnp.stack(mine), ('row', 'col'))  145 us
    all_gather x1, waiting for transfers between devices, leading_factor(): grid = lax.all_gather(first[0], ('row', 'col'), axis=0)  70.4 us
    psum x1, waiting for transfers between devices, shards(): lax.psum(jnp.where(root, chosen, jnp.zeros((), jnp.float32)), 'row')  63 us
    unnamed x222, local copies, waits for them, and re-layouts  46.6 us
    dot_general x22, matrix products, dot_t(): return lax.dot_general(a, b, (((1,), (1,)), ((), ())), precision=HIGH)  37.8 us
    dot_general x84, matrix products, dot(): return jnp.dot(a, b, precision=HIGH)  33.9 us
  transfers between devices with their start and end apart: 5, of which 3 were waited for; matrix products, arithmetic and copies ran while one was open for 46% of the time, Pallas kernels for 0%

profile of v1, /device:TPU:0, one launch (start us, length us, event | category | flops | bytes accessed | tf_op | source)
XLA Modules:
  0.0 750.1 jit_solution(17167165850774572412)
XLA Ops:
  6.5 6.2 copy.151
  16.1 2.8 gather_fusion
  19.0 4.5 broadcast_select_fusion
  23.4 7.4 all-to-all-start
  30.9 2.5 slice.278
  34.3 2.4 copy.245
  37.5 144.8 %all-reduce.4.cloned.1.call-done = f32[3,256,256]{1,2,0:T(8,128)} async-done(((f32[3,256,256]{1,2,0:T(8,128)}), f32[3,256,256]{1,2,0:T(8,128)}) %all-reduce.4.cloned.1.call-update) | async-done | bytes 786448 | tf_op jit(solution)/shard_map/psum | solution.py:47
  182.3 1.9 slice_bitcast_fusion.2
  184.2 4.9 fusion.8
  191.7 70.4 %all-gather.5.cloned.1.call-done = f32[32,256,1,256]{3,1,2,0:T(8,128)} async-done(((f32[1,256,1,256]{3,1,2,0:T(8,128)}), f32[32,256,1,256]{3,1,2,0:T(8,128)}) %all-gather.5.cloned.1.call-update) | async-done | bytes 8388624 | tf_op jit(solution)/shard_map/all_gather | solution.py:34
  262.2 3.2 slice_bitcast_fusion.5
  276.3 11.7 %cholesky.298 = f32[128,128]{1,0:T(8,128)S(1)} custom-call(f32[128,128]{1,0:T(8,128)S(1)} %copy.154), custom_call_target="Cholesky" | custom-call | tf_op jit(solution)/shard_map/jit(cholesky)/cholesky | solution.py:68
  288.8 9.8 %custom-call.13 = f32[1,128,128]{1,2,0:T(8,128)S(1)} custom-call(f32[1,128,128]{2,1,0:T(8,128)S(1)} %get-tuple-element.105), custom_call_target="InvertDiagBlocksLowerTriangular" | custom-call | tf_op jit(solution)/shard_map/jit(cholesky)/cholesky | solution.py:68
  299.3 11.7 %cholesky.315 = f32[128,128]{1,0:T(8,128)S(1)} custom-call(f32[128,128]{1,0:T(8,128)S(1)} %copy.156), custom_call_target="Cholesky" | custom-call | tf_op jit(solution)/shard_map/jit(cholesky)/cholesky | solution.py:68
  320.6 11.7 %cholesky.332 = f32[128,128]{1,0:T(8,128)S(1)} custom-call(f32[128,128]{1,0:T(8,128)S(1)} %cholesky.501), custom_call_target="Cholesky" | custom-call | tf_op jit(solution)/shard_map/jit(cholesky)/cholesky | solution.py:68
  333.0 9.8 %custom-call.14 = f32[1,128,128]{1,2,0:T(8,128)S(1)} custom-call(f32[1,128,128]{2,1,0:T(8,128)S(1)} %get-tuple-element.101), custom_call_target="InvertDiagBlocksLowerTriangular" | custom-call | tf_op jit(solution)/shard_map/jit(cholesky)/cholesky | solution.py:68
  343.3 11.9 %cholesky.349 = f32[128,128]{1,0:T(8,128)S(1)} custom-call(f32[128,128]{1,0:T(8,128)S(1)} %convolution_subtract_fusion.9), custom_call_target="Cholesky" | custom-call | tf_op jit(solution)/shard_map/jit(cholesky)/cholesky | solution.py:68
  366.5 2.0 fusion.103
  370.4 1.9 copy.224
  372.5 1.4 constant_dynamic-update-slice_fusion.3
  377.5 11.9 %cholesky.366 = f32[128,128]{1,0:T(8,128)S(1)} custom-call(f32[128,128]{1,0:T(8,128)S(1)} %cholesky.504), custom_call_target="Cholesky" | custom-call | tf_op jit(solution)/shard_map/jit(cholesky)/cholesky | solution.py:68
  390.1 9.8 %custom-call.15 = f32[1,128,128]{1,2,0:T(8,128)S(1)} custom-call(f32[1,128,128]{2,1,0:T(8,128)S(1)} %get-tuple-element.97), custom_call_target="InvertDiagBlocksLowerTriangular" | custom-call | tf_op jit(solution)/shard_map/jit(cholesky)/cholesky | solution.py:68
  400.4 11.7 %cholesky.383 = f32[128,128]{1,0:T(8,128)S(1)} custom-call(f32[128,128]{1,0:T(8,128)S(1)} %convolution_subtract_fusion.8), custom_call_target="Cholesky" | custom-call | tf_op jit(solution)/shard_map/jit(cholesky)/cholesky | solution.py:68
  415.8 1.8 copy.179
  417.8 1.3 convolution_add_fusion.26
  423.5 1.5 fusion.91
  426.7 1.8 copy.183
  430.3 11.7 %cholesky.400 = f32[128,128]{1,0:T(8,128)S(1)} custom-call(f32[128,128]{1,0:T(8,128)S(1)} %cholesky.507), custom_call_target="Cholesky" | custom-call | tf_op jit(solution)/shard_map/jit(cholesky)/cholesky | solution.py:68
  443.4 9.8 %custom-call.16 = f32[1,128,128]{1,2,0:T(8,128)S(1)} custom-call(f32[1,128,128]{2,1,0:T(8,128)S(1)} %get-tuple-element.93), custom_call_target="InvertDiagBlocksLowerTriangular" | custom-call | tf_op jit(solution)/shard_map/jit(cholesky)/cholesky | solution.py:68
  453.2 1.7 constant_dynamic-update-slice_fusion.20
  456.0 11.7 %cholesky.417 = f32[128,128]{1,0:T(8,128)S(1)} custom-call(f32[128,128]{1,0:T(8,128)S(1)} %convolution_subtract_fusion.7), custom_call_target="Cholesky" | custom-call | tf_op jit(solution)/shard_map/jit(cholesky)/cholesky | solution.py:68
  480.9 1.8 copy.187
  484.5 11.7 %cholesky.434 = f32[128,128]{1,0:T(8,128)S(1)} custom-call(f32[128,128]{1,0:T(8,128)S(1)} %cholesky.510), custom_call_target="Cholesky" | custom-call | tf_op jit(solution)/shard_map/jit(cholesky)/cholesky | solution.py:68
  497.6 9.8 %custom-call.17 = f32[1,128,128]{1,2,0:T(8,128)S(1)} custom-call(f32[1,128,128]{2,1,0:T(8,128)S(1)} %get-tuple-element.89), custom_call_target="InvertDiagBlocksLowerTriangular" | custom-call | tf_op jit(solution)/shard_map/jit(cholesky)/cholesky | solution.py:68
  507.4 1.7 constant_dynamic-update-slice_fusion.18
  510.2 11.9 %cholesky.451 = f32[128,128]{1,0:T(8,128)S(1)} custom-call(f32[128,128]{1,0:T(8,128)S(1)} %convolution_subtract_fusion.6), custom_call_target="Cholesky" | custom-call | tf_op jit(solution)/shard_map/jit(cholesky)/cholesky | solution.py:68
  530.3 1.8 copy.217
  533.4 1.4 convolution_add_fusion.10
  537.3 2.4 convolution_subtract_fusion.4
  539.7 1.8 copy.191
  543.3 11.7 %cholesky.468 = f32[128,128]{1,0:T(8,128)S(1)} custom-call(f32[128,128]{1,0:T(8,128)S(1)} %cholesky.513), custom_call_target="Cholesky" | custom-call | tf_op jit(solution)/shard_map/jit(cholesky)/cholesky | solution.py:68
  555.8 10.2 %custom-call.18 = f32[1,128,128]{1,2,0:T(8,128)S(1)} custom-call(f32[1,128,128]{2,1,0:T(8,128)S(1)} %get-tuple-element.85), custom_call_target="InvertDiagBlocksLowerTriangular" | custom-call | tf_op jit(solution)/shard_map/jit(cholesky)/cholesky | solution.py:68
  566.0 1.7 constant_dynamic-update-slice_fusion.16
  568.8 11.7 %cholesky.485 = f32[128,128]{1,0:T(8,128)S(1)} custom-call(f32[128,128]{1,0:T(8,128)S(1)} %convolution_subtract_fusion.5), custom_call_target="Cholesky" | custom-call | tf_op jit(solution)/shard_map/jit(cholesky)/cholesky | solution.py:68
  591.4 1.4 fusion.81
  599.2 4.8 slice.348
  604.0 4.7 gather_fusion.1
  608.8 3.8 select_bitcast_fusion
  612.6 1.9 dynamic-slice_bitcast_fusion.1
  616.8 63.0 %all-reduce.6.cloned.1.call-done = f32[6,2,256,256]{3,2,0,1:T(8,128)} async-done(((f32[6,2,256,256]{3,2,0,1:T(8,128)}), f32[6,2,256,256]{3,2,0,1:T(8,128)}) %all-reduce.6.cloned.1.call-update) | async-done | bytes 3145744 | tf_op jit(solution)/shard_map/psum | solution.py:122
  679.8 3.7 pad_maximum_fusion
  686.7 2.3 convolution_subtract_fusion
  690.1 3.3 fusion.19
  694.6 4.6 fusion.22
  700.0 5.4 convolution_subtract_fusion.3
  706.2 4.2 fusion.17
  710.4 2.4 slice.359
  712.9 6.0 copy.198
  718.9 2.2 reshape.208
  721.1 6.9 reshape.207
  728.0 3.7 constant_dynamic-slice_fusion
  732.3 3.9 fusion.48
  738.2 1.4 maximum_bitcast_fusion
  739.6 3.5 copy.201
  (429 shorter events, 115.6 us)
Async XLA Ops:
  6.5 9.6 %copy-start = (bf16[1,16,256,256]{3,2,1,0:T(8,128)(2,1)S(1)}, bf16[1,16,256,256]{3,2,1,0:T(8,128)(2,1)}, u32[]{:S(2)}) copy-start(bf16[1,16,256,256]{3,2,1,0:T(8,128)(2,1)} %param.5) | copy-start | bytes 6291460
  6.5 175.8 %all-reduce.4.cloned.1.call-start = ((), (), s32[]{:S(2)}) async-start(), calls=%async_computation.1 | async-start | bytes 1572864 | tf_op jit(solution)/shard_map/psum | solution.py:47
  13.8 1.9 copy-start.91
  14.8 247.4 %all-gather.5.cloned.1.call-start = ((), (), s32[]{:S(2)}) async-start(), calls=%async_computation.3 | async-start | bytes 8650752 | tf_op jit(solution)/shard_map/all_gather | solution.py:34
  23.4 160.8 %all-to-all-start = ((bf16[32,256,256]{2,1,0:T(8,128)(2,1)}), bf16[32,256,256]{2,1,0:T(8,128)(2,1)}, u32[]{:S(2)}, u32[]{:S(2)}) async-start(bf16[32,256,256]{2,1,0:T(8,128)(2,1)} %broadcast_select_fusion), calls=%async_computation | async-start | bytes 8388608 | tf_op jit(solution)/shard_map/all_to_all | solution.py:107
  30.9 568.4 %all-gather.7.cloned.1.call-start = ((), (), s32[]{:S(2)}) async-start(), calls=%async_computation.4 | async-start | bytes 7077888 | tf_op jit(solution)/shard_map/all_gather | solution.py:118
  33.4 3.3 copy-start.2
  184.2 4.9 copy-start.7
  189.1 1.3 copy-start.4
  191.5 488.3 %all-reduce.6.cloned.1.call-start = ((), (), s32[]{:S(2)}) async-start(), calls=%async_computation.2 | async-start | bytes 6291456 | tf_op jit(solution)/shard_map/psum | solution.py:122
  276.2 11.8 %copy-start.32 = (f32[1280,256]{0,1:T(8,128)}, f32[1280,256]{0,1:T(8,128)S(1)}, u32[]{:S(2)}) copy-start(f32[1280,256]{0,1:T(8,128)S(1)} %get-tuple-element.25) | copy-start | bytes 3932164
  318.1 2.2 copy-start.30
  318.1 1.4 copy-start.33
  366.2 2.3 copy-start.47
  366.5 3.9 copy-start.24
  366.5 5.8 copy-start.46
  370.4 3.6 copy-start.19
  372.4 2.8 copy-start.17
  372.5 1.6 copy-start.48
  372.5 1.6 copy-start.53
  372.5 1.6 copy-start.79
  372.5 1.6 copy-start.80
  372.5 1.6 copy-start.86
  372.5 1.7 copy-start.87
  374.0 1.3 copy-start.40
  374.0 1.3 copy-start.63
  374.0 1.3 copy-start.67
  374.0 1.3 copy-start.81
  412.2 3.6 copy-start.10
  420.6 1.2 copy-start.35
  421.9 1.3 copy-start.64
  421.9 1.3 copy-start.68
  421.9 1.4 copy-start.77
  421.9 1.5 copy-start.78
  421.9 1.5 copy-start.82
  421.9 1.6 copy-start.88
  422.8 2.2 copy-start.70
  422.9 2.2 copy-start.73
  422.9 2.2 copy-start.84
  470.4 2.7 copy-start.12
  475.6 1.2 copy-start.37
  476.5 1.8 copy-start.21
  476.5 1.8 copy-start.50
  476.5 1.8 copy-start.65
  476.5 1.8 copy-start.71
  476.5 1.8 copy-start.83
  476.5 1.8 copy-start.85
  476.5 1.8 copy-start.89
  476.5 1.8 copy-start.90
  476.8 1.4 copy-start.28
  524.7 2.7 copy-start.14
  583.7 3.0 copy-start.51
  583.7 3.1 copy-start.5
  591.1 1.7 copy-start.43
  591.1 1.7 copy-start.45
  616.8 66.7 %copy-start.31 = (f32[256,256]{1,0:T(8,128)S(1)}, f32[256,256]{1,0:T(8,128)}, u32[]{:S(2)}) copy-start(f32[256,256]{1,0:T(8,128)} %copy-done.30) | copy-start | bytes 786436
  684.4 1.3 copy-start.25
  686.7 2.3 copy-start.27
  690.1 3.3 copy-start.29
  694.6 4.6 copy-start.23
  700.0 5.4 copy-start.59
  728.0 4.2 copy-start.3
  728.0 4.2 copy-start.6
  738.2 4.9 copy-start.1
  (33 other events, 33.1 us)
Sparse Core Ops, SparseCore 0:
  14.9 167.3 all-reduce.3
  185.7 76.4 all-gather.4
  264.6 97.7 all-gather.6
  612.7 67.0 all-reduce.5

commit v2 on v1

--- a/solution.py
+++ b/solution.py
@@ -21,32 +21,36 @@
     inv_diag = 1.0 / jnp.sum(lower * eye, axis=0)
     power = eye - lower * inv_diag[None, :]
     result = eye + power
+    power = dot(power, power)
     reach = 2
-    while reach < size:
-        power = dot(power, power)
-        result = result + dot(result, power)
+    while 2 * reach < size:
+        both = dot(jnp.concatenate([result, power], axis=0), power)
+        result = result + both[:size]
+        power = both[size:]
         reach *= 2
+    result = result + dot(result, power)
     return result * inv_diag[:, None]
 
 
-def leading_factor(first, row_count, col_count, my_row, my_col):
-    tile = first.shape[1]
-    grid = lax.all_gather(first[0], ("row", "col"), axis=0)
+def tile_factor(pivot):
+    half = pivot.shape[0] // 2
+    low1 = lax.linalg.cholesky(pivot[:half, :half], symmetrize_input=False)
+    inv1 = lower_inverse(low1)
+    below = dot_t(pivot[half:, :half], inv1)
+    low2 = lax.linalg.cholesky(pivot[half:, half:] - dot_t(below, below), symmetrize_input=False)
+    inv2 = lower_inverse(low2)
+    zero = jnp.zeros((half, half), jnp.float32)
+    corner = -dot(inv2, dot(below, inv1))
+    lower = jnp.block([[low1, zero], [below, low2]])
+    inverse = jnp.block([[inv1, zero], [corner, inv2]])
+    return lower, inverse
+
+
+def leading_factor(first, extra, row_count, col_count):
+    tile = first.shape[0]
+    grid = lax.all_gather(first, ("row", "col"), axis=0)
     grid = grid.reshape(row_count, col_count, tile, tile)
     pairs = [(i, j) for j in range(row_count, PANELS) for i in range(j, PANELS)]
-    extra = {}
-    if pairs:
-        mine = [
-            jnp.where(
-                (my_row == i % row_count) & (my_col == j),
-                first[i // row_count],
-                jnp.zeros((), jnp.float32),
-            )
-            for i, j in pairs
-        ]
-        summed = lax.psum(jnp.stack(mine), ("row", "col"))
-        extra = {pair: summed[n] for n, pair in enumerate(pairs)}
-
     def tile_at(i, j):
         if i < row_count:
             return grid[i, j]
@@ -65,8 +69,7 @@
             )
             column = column - dot_t(left, left[:tile])
         pivot = column[:tile]
-        lower = jnp.linalg.cholesky(pivot)
-        inverse = lower_inverse(lower)
+        lower, inverse = tile_factor(pivot)
         inverses.append(inverse)
         lead[k, k] = lower
         if k + 1 < PANELS:
@@ -89,8 +92,6 @@
     front = parent_front.reshape(lrows, tile, lcols, tile)
     first = PANELS // row_count
     lead_rows = -(-PANELS // row_count)
-
-    lead, inverses = leading_factor(front[:lead_rows, :, 0, :], row_count, col_count, my_row, my_col)
 
     stored = child_tiles.shape[1]
     held = child_tiles.reshape(stored, tile, tile)
@@ -117,9 +118,38 @@
 
     panel = lax.all_gather(lower_front[:, 0], "col", axis=0)[:PANELS]
     pick = my_col // row_count + col_count // row_count * jnp.arange(lcols, dtype=jnp.int32) - first
-    chosen = panel[:, jnp.clip(pick, 0, count - 1)]
+    source = panel[:, jnp.clip(pick, 0, count - 1)]
     root = my_row == my_col % row_count
-    chosen = lax.psum(jnp.where(root, chosen, jnp.zeros((), jnp.float32)), "row")
+    parts = []
+    for j in range(lcols):
+        own = source[:, j]
+        total = jnp.where(root, own, 0.0)
+        for shift in range(1, row_count):
+            pairs = [
+                (c % row_count * col_count + c, (c + shift) % row_count * col_count + c)
+                for c in range(col_count)
+                if c + j * col_count >= PANELS
+            ]
+            total = total + lax.ppermute(own, ("row", "col"), pairs)
+        parts.append(total)
+    chosen = jnp.stack(parts, axis=1)
+
+    extra = {}
+    if PANELS > row_count:
+        corner = panel[row_count:, 0]
+        holders = PANELS - row_count
+        received = [corner] + [
+            lax.ppermute(corner, "row", [(r, (r + shift) % row_count) for r in range(holders)])
+            for shift in range(1, row_count)
+        ]
+        for r in range(holders):
+            full = received[0]
+            for shift in range(1, row_count):
+                full = jnp.where((my_row - r) % row_count == shift, received[shift], full)
+            for j in range(r + 1):
+                extra[row_count + r, row_count + j] = full[j]
+    lead, inverses = leading_factor(front[0, :, 0, :], extra, row_count, col_count)
+
     stack = jnp.concatenate([panel, chosen], axis=1).reshape(PANELS, (count + lcols) * tile, tile)
     solved = []
     for k in range(PANELS):

time: 758 us -> 586 us (0.77)
  waiting for transfers between devices: 278 us -> 133 us
  other arithmetic: 243 us -> 195 us
  starting transfers between devices: 7.76 us -> 28.4 us
  local copies, waits for them, and re-layouts: 110 us -> 125 us
    psum x2 -> x0, waiting for transfers between devices: 208 us -> none  [the longest x1 145 us: leading_factor(): summed = lax.psum(jnp.stack(mine), ('row', 'col'))]
    all_to_all x1, waiting for transfers between devices: 0.01 us -> 126 us  [shards(): lax.all_to_all(outgoing, ('row', 'col'), split_axis=0, concat_axis=0, til...]
    all_gather x1, waiting for transfers between devices: 70.4 us -> 0.02 us  [leading_factor(): grid = lax.all_gather(first, ('row', 'col'), axis=0)]
    another operation x43 -> x37, other arithmetic: 212 us -> 159 us  [the longest x18 77.6 us: tile_factor(): lax.linalg.cholesky(pivot[half:, half:] - dot_t(below, below), symmetrize...]
    ppermute x0 -> x9, starting transfers between devices: none -> 21 us  [the longest x6 14.5 us: shards(): total = total + lax.ppermute(own, ('row', 'col'), pairs)]
    dot_general x22 -> x34, matrix products: 37.8 us -> 48.3 us  [dot_t(): return lax.dot_general(a, b, (((1,), (1,)), ((), ())), precision=HIGH)]
    another operation x12 -> x0, matrix products: 9.84 us -> none  [leading_factor(): lower = jnp.linalg.cholesky(pivot)]
    all_gather x0 -> x1, local copies, waits for them, and re-layouts: none -> 9.49 us  [leading_factor(): grid = lax.all_gather(first, ('row', 'col'), axis=0)]
  transfers between devices with their start and end apart: 5 -> 12, of which waited for: 3 -> 2; matrix products, arithmetic and copies ran while one was open for 46% -> 55% of each run, Pallas kernels for 0% -> 0%
where the time goes in v2:
time: 586 us; the launch traced here: 577 us
  other arithmetic  195 us (33%)
  waiting for transfers between devices  133 us (23%)
  local copies, waits for them, and re-layouts  125 us (21%)
  matrix products  79 us (13%)
  starting transfers between devices  28.4 us (5%)
  between operations  17.5 us (3%)
    all_to_all x1, waiting for transfers between devices, shards(): lax.all_to_all(outgoing, ('row', 'col'), split_axis=0, concat_axis=0, til...  126 us
    another operation x18, other arithmetic, tile_factor(): lax.linalg.cholesky(pivot[half:, half:] - dot_t(below, below), symmetrize...  77.6 us
    another operation x18, other arithmetic, tile_factor(): low1 = lax.linalg.cholesky(pivot[:half, :half], symmetrize_input=False)  76.8 us
    dot_general x34, matrix products, dot_t(): return lax.dot_general(a, b, (((1,), (1,)), ((), ())), precision=HIGH)  48.3 us
    unnamed x271, local copies, waits for them, and re-layouts  43.1 us
    dot_general x96, matrix products, dot(): return jnp.dot(a, b, precision=HIGH)  25.8 us
    ppermute x6, starting transfers between devices, shards(): total = total + lax.ppermute(own, ('row', 'col'), pairs)  14.5 us
  transfers between devices with their start and end apart: 12, of which 2 were waited for; matrix products, arithmetic and copies ran while one was open for 55% of the time, Pallas kernels for 0%

profile of v2, /device:TPU:0, one launch (start us, length us, event | category | flops | bytes accessed | tf_op | source)
XLA Modules:
  0.0 576.9 jit_solution(10294276750164803854)
XLA Ops:
  6.5 1.9 copy.312
  9.6 2.8 gather_fusion
  12.5 4.5 broadcast_select_fusion
  17.0 7.4 %all-to-all-start = ((bf16[32,256,256]{2,1,0:T(8,128)(2,1)}), bf16[32,256,256]{2,1,0:T(8,128)(2,1)}, u32[]{:S(2)}, u32[]{:S(2)}) async-start(bf16[32,256,256]{2,1,0:T(8,128)(2,1)} %broadcast_select_fusion), calls=%async_computation | async-start | bytes 8388608 | tf_op jit(solution)/shard_map/all_to_all | solution.py:108
  24.5 2.5 slice.753
  27.8 2.4 copy.311
  31.0 126.3 %all-to-all-done = bf16[32,256,256]{2,1,0:T(8,128)(2,1)} async-done(((bf16[32,256,256]{2,1,0:T(8,128)(2,1)}), bf16[32,256,256]{2,1,0:T(8,128)(2,1)}, u32[]{:S(2)}, u32[]{:S(2)}) %all-to-all-start) | async-done | bytes 4194336 | tf_op jit(solution)/shard_map/all_to_all | solution.py:108
  157.3 4.9 fusion.8
  164.6 1.9 slice_bitcast_fusion.11
  167.6 9.5 %copy.190 = f32[32,256,1,256]{1,3,0,2:T(8,128)} copy(f32[32,256,1,256]{3,1,2,0:T(8,128)} %all-gather.5.cloned.1.call-done) | data formatting | bytes 16777216 | tf_op jit(solution)/shard_map/all_gather | solution.py:51
  177.1 2.5 slice_bitcast_fusion.7
  179.6 11.7 %custom-call.14 = f32[128,128]{1,0:T(8,128)S(1)} custom-call(f32[128,128]{1,0:T(8,128)S(1)} %copy.191), custom_call_target="Cholesky" | custom-call | tf_op jit(solution)/shard_map/cholesky/custom-call.1 | solution.py:37
  194.9 11.7 %custom-call.15 = f32[128,128]{1,0:T(8,128)S(1)} custom-call(f32[128,128]{1,0:T(8,128)S(1)} %copy.194), custom_call_target="Cholesky" | custom-call | tf_op jit(solution)/shard_map/cholesky/custom-call.1 | solution.py:40
  218.2 11.7 %custom-call.16 = f32[128,128]{1,0:T(8,128)S(1)} custom-call(f32[128,128]{1,0:T(8,128)S(1)} %slice.866), custom_call_target="Cholesky" | custom-call | tf_op jit(solution)/shard_map/cholesky/custom-call.1 | solution.py:37
  234.3 11.7 %custom-call.17 = f32[128,128]{1,0:T(8,128)S(1)} custom-call(f32[128,128]{1,0:T(8,128)S(1)} %convolution_subtract_fusion.4), custom_call_target="Cholesky" | custom-call | tf_op jit(solution)/shard_map/cholesky/custom-call.1 | solution.py:40
  252.7 1.7 fusion.96
  256.4 1.9 copy.286
  262.7 11.7 %custom-call.18 = f32[128,128]{1,0:T(8,128)S(1)} custom-call(f32[128,128]{1,0:T(8,128)S(1)} %slice.902), custom_call_target="Cholesky" | custom-call | tf_op jit(solution)/shard_map/cholesky/custom-call.1 | solution.py:37
  279.7 11.7 %custom-call.19 = f32[128,128]{1,0:T(8,128)S(1)} custom-call(f32[128,128]{1,0:T(8,128)S(1)} %convolution_subtract_fusion.3), custom_call_target="Cholesky" | custom-call | tf_op jit(solution)/shard_map/cholesky/custom-call.1 | solution.py:40
  295.8 1.8 fusion.100
  300.7 13.2 %custom-call.20 = f32[128,128]{1,0:T(8,128)} custom-call(f32[128,128]{1,0:T(8,128)} %slice.932), custom_call_target="Cholesky" | custom-call | tf_op jit(solution)/shard_map/cholesky/custom-call.1 | solution.py:37
  315.4 2.1 fusion.448
  320.6 1.6 copy.219
  322.2 1.8 copy.283
  328.7 1.7 fusion.416
  331.9 1.8 convolution_subtract_fusion.2
  333.7 13.2 %custom-call.21 = f32[128,128]{1,0:T(8,128)} custom-call(f32[128,128]{1,0:T(8,128)} %convolution_subtract_fusion.2), custom_call_target="Cholesky" | custom-call | tf_op jit(solution)/shard_map/cholesky/custom-call.1 | solution.py:40
  356.9 1.7 bitcast_dynamic-update-slice_fusion.8
  368.9 1.9 slice_bitcast_fusion.2
  370.8 2.2 collective-permute-start.2
  373.0 2.3 collective-permute-start.1
  375.3 1.9 collective-permute-start
  378.1 4.9 slice.1005
  383.0 4.8 gather_fusion.1
  387.8 3.8 slice_bitcast_fusion.1
  391.6 1.8 collective-permute-start.4
  393.5 1.8 collective-permute-start.3
  395.3 1.8 collective-permute-start.5
  397.1 2.5 collective-permute-start.7
  399.5 4.1 collective-permute-start.6
  408.7 11.7 %custom-call.22 = f32[128,128]{1,0:T(8,128)S(1)} custom-call(f32[128,128]{1,0:T(8,128)S(1)} %slice.967), custom_call_target="Cholesky" | custom-call | tf_op jit(solution)/shard_map/cholesky/custom-call.1 | solution.py:37
  426.0 1.7 convolution_subtract_fusion.1
  427.7 12.5 %custom-call.23 = f32[128,128]{1,0:T(8,128)S(1)} custom-call(f32[128,128]{1,0:T(8,128)} %convolution_subtract_fusion.1), custom_call_target="Cholesky" | custom-call | tf_op jit(solution)/shard_map/cholesky/custom-call.1 | solution.py:40
  448.1 2.0 constant_dynamic-update-slice_fusion
  451.8 11.7 %custom-call.24 = f32[128,128]{1,0:T(8,128)S(1)} custom-call(f32[128,128]{1,0:T(8,128)S(1)} %slice.992), custom_call_target="Cholesky" | custom-call | tf_op jit(solution)/shard_map/cholesky/custom-call.1 | solution.py:37
  466.8 11.7 %custom-call.25 = f32[128,128]{1,0:T(8,128)S(1)} custom-call(f32[128,128]{1,0:T(8,128)S(1)} %slice_subtract_fusion), custom_call_target="Cholesky" | custom-call | tf_op jit(solution)/shard_map/cholesky/custom-call.1 | solution.py:40
  484.3 2.5 collective-permute-start.8
  489.3 2.8 bitcast_dynamic-update-slice_fusion.1
  492.1 2.9 bitcast_dynamic-update-slice_fusion
  495.0 1.9 dynamic-slice_bitcast_fusion.1
  497.6 6.2 %collective-permute-done.8 = f32[6,256,256]{2,1,0:T(8,128)} collective-permute-done((f32[6,256,256]{2,1,0:T(8,128)}, f32[6,256,256]{2,1,0:T(8,128)}, u32[]{:S(2)}, u32[]{:S(2)}) %collective-permute-start.8) | collective-permute-done | bytes 1572896 | tf_op jit(solution)/shard_map/ppermute | solution.py:133
  503.8 4.6 add_bitcast_fusion.1
  513.5 2.3 bitcast_subtract_fusion.3
  516.9 3.3 bitcast_subtract_fusion.2
  521.4 4.8 bitcast_subtract_fusion.1
  527.0 5.4 bitcast_subtract_fusion
  533.1 4.2 fusion.17
  537.3 2.5 slice.1024
  539.8 6.1 %copy.251 = f32[768,1536]{1,0:T(8,128)} copy(f32[768,1536]{0,1:T(8,128)} %slice.1024) | data formatting | bytes 9437184 | tf_op jit(solution)/shard_map/slice | solution.py:169
  545.9 2.2 reshape.195
  548.0 6.9 %reshape.194 = f32[3,256,6,256]{3,2,1,0:T(8,128)} reshape(f32[768,1536]{1,0:T(8,128)} %copy.251) | data formatting | bytes 9437184 | tf_op jit(solution)/shard_map/reshape | solution.py:169
  554.9 3.7 constant_dynamic-slice_fusion
  559.1 3.9 fusion.43
  566.4 3.5 copy.254
  (567 shorter events, 125.5 us)
Async XLA Ops:
  6.5 3.1 copy-start
  6.5 2.7 copy-start.116
  6.5 158.1 %all-gather.5.cloned.1.call-start = ((), (), s32[]{:S(2)}) async-start(), calls=%async_computation.1 | async-start | bytes 8650752 | tf_op jit(solution)/shard_map/all_gather | solution.py:51
  17.0 140.3 %all-to-all-start = ((bf16[32,256,256]{2,1,0:T(8,128)(2,1)}), bf16[32,256,256]{2,1,0:T(8,128)(2,1)}, u32[]{:S(2)}, u32[]{:S(2)}) async-start(bf16[32,256,256]{2,1,0:T(8,128)(2,1)} %broadcast_select_fusion), calls=%async_computation | async-start | bytes 8388608 | tf_op jit(solution)/shard_map/all_to_all | solution.py:108
  24.4 344.5 %all-gather.7.cloned.1.call-start = ((), (), s32[]{:S(2)}) async-start(), calls=%async_computation.2 | async-start | bytes 7077888 | tf_op jit(solution)/shard_map/all_gather | solution.py:119
  27.0 3.2 copy-start.3
  157.3 4.9 copy-start.8
  194.5 14.9 %copy-start.25 = (f32[128,128]{1,0:T(8,128)}, f32[128,128]{1,0:T(8,128)S(1)}, u32[]{:S(2)}) copy-start(f32[128,128]{1,0:T(8,128)S(1)} %fusion.427) | copy-start | bytes 196612
  210.0 5.5 copy-start.39
  215.5 2.7 copy-start.69
  233.0 19.7 %copy-start.17 = (f32[128,128]{1,0:T(8,128)}, f32[128,128]{1,0:T(8,128)S(1)}, u32[]{:S(2)}) copy-start(f32[128,128]{1,0:T(8,128)S(1)} %fusion.86) | copy-start | bytes 196612
  233.2 12.9 %copy-start.29 = (f32[128,128]{0,1:T(8,128)}, f32[128,128]{0,1:T(8,128)S(1)}, u32[]{:S(2)}) copy-start(f32[128,128]{0,1:T(8,128)S(1)} %fusion.424) | copy-start | bytes 196612
  251.6 4.7 copy-start.41
  252.7 2.5 copy-start.71
  256.3 3.6 copy-start.12
  258.4 3.2 copy-start.9
  276.4 16.6 %copy-start.49 = (f32[256,256]{0,1:T(8,128)S(1)}, f32[256,256]{0,1:T(8,128)}, u32[]{:S(2)}) copy-start(f32[256,256]{0,1:T(8,128)} %get-tuple-element.35) | copy-start | bytes 786436
  278.4 13.1 %copy-start.34 = (f32[128,128]{0,1:T(8,128)}, f32[128,128]{0,1:T(8,128)S(1)}, u32[]{:S(2)}) copy-start(f32[128,128]{0,1:T(8,128)S(1)} %fusion.420) | copy-start | bytes 196612
  292.8 2.0 copy-start.30
  295.5 2.1 copy-start.37
  295.7 1.9 copy-start.67
  295.7 2.0 copy-start.13
  295.7 2.0 copy-start.52
  295.7 2.0 copy-start.57
  295.7 2.0 copy-start.87
  295.7 2.0 copy-start.91
  295.7 2.0 copy-start.100
  295.7 2.0 copy-start.101
  295.7 2.0 copy-start.103
  295.7 2.0 copy-start.112
  354.9 3.7 copy-start.10
  354.9 3.7 copy-start.58
  354.9 3.8 copy-start.53
  354.9 4.5 copy-start.6
  362.0 3.1 copy-start.43
  362.4 2.6 copy-start.73
  362.9 2.2 copy-start.50
  370.8 24.5 %collective-permute-start.2 = (f32[2,256,256]{2,1,0:T(8,128)}, f32[2,256,256]{2,1,0:T(8,128)}, u32[]{:S(2)}, u32[]{:S(2)}) collective-permute-start(f32[2,256,256]{2,1,0:T(8,128)} %slice_bitcast_fusion.2), channel_id=1, source_target_pairs={{0,8},{8,16},{1,9},{9,17},{2,10},{10,18},{3,11},{11,19},{4,12},{12... | collective-permute-start | bytes 1572872 | tf_op jit(solution)/shard_map/ppermute | solution.py:142
  373.0 24.1 %collective-permute-start.1 = (f32[2,256,256]{2,1,0:T(8,128)}, f32[2,256,256]{2,1,0:T(8,128)}, u32[]{:S(2)}, u32[]{:S(2)}) collective-permute-start(f32[2,256,256]{2,1,0:T(8,128)} %slice_bitcast_fusion.2), channel_id=1, source_target_pairs={{0,16},{8,24},{1,17},{9,25},{2,18},{10,26},{3,19},{11,27},{4,20},{... | collective-permute-start | bytes 1572872 | tf_op jit(solution)/shard_map/ppermute | solution.py:142
  375.3 24.2 %collective-permute-start = (f32[2,256,256]{2,1,0:T(8,128)}, f32[2,256,256]{2,1,0:T(8,128)}, u32[]{:S(2)}, u32[]{:S(2)}) collective-permute-start(f32[2,256,256]{2,1,0:T(8,128)} %slice_bitcast_fusion.2), channel_id=1, source_target_pairs={{0,24},{8,0},{1,25},{9,1},{2,26},{10,2},{3,27},{11,3},{4,28},{12,4... | collective-permute-start | bytes 1572872 | tf_op jit(solution)/shard_map/ppermute | solution.py:142
  391.6 92.7 %collective-permute-start.4 = (f32[6,256,256]{2,1,0:T(8,128)}, f32[6,256,256]{2,1,0:T(8,128)}, u32[]{:S(2)}, u32[]{:S(2)}) collective-permute-start(f32[6,256,256]{2,1,0:T(8,128)} %get-tuple-element.61), channel_id=1, source_target_pairs={{22,6},{31,15}} | collective-permute-start | bytes 4718600 | tf_op jit(solution)/shard_map/ppermute | solution.py:133
  393.5 104.1 %collective-permute-start.3 = (f32[6,256,256]{2,1,0:T(8,128)}, f32[6,256,256]{2,1,0:T(8,128)}, u32[]{:S(2)}, u32[]{:S(2)}) collective-permute-start(f32[6,256,256]{2,1,0:T(8,128)} %get-tuple-element.61), channel_id=1, source_target_pairs={{22,30},{31,7}} | collective-permute-start | bytes 4718600 | tf_op jit(solution)/shard_map/ppermute | solution.py:133
  395.3 102.3 %collective-permute-start.5 = (f32[6,256,256]{2,1,0:T(8,128)}, f32[6,256,256]{2,1,0:T(8,128)}, u32[]{:S(2)}, u32[]{:S(2)}) collective-permute-start(f32[6,256,256]{2,1,0:T(8,128)} %get-tuple-element.61), channel_id=1, source_target_pairs={{22,14},{31,23}} | collective-permute-start | bytes 4718600 | tf_op jit(solution)/shard_map/ppermute | solution.py:133
  397.1 100.6 %collective-permute-start.7 = (f32[6,256,256]{2,1,0:T(8,128)}, f32[6,256,256]{2,1,0:T(8,128)}, u32[]{:S(2)}, u32[]{:S(2)}) collective-permute-start(f32[6,256,256]{2,1,0:T(8,128)} %get-tuple-element.62), channel_id=1, source_target_pairs={{0,16},{9,25},{18,2},{27,11},{4,20},{13,29},{22,6},{31,15}} | collective-permute-start | bytes 4718600 | tf_op jit(solution)/shard_map/ppermute | solution.py:133
  399.5 98.1 %collective-permute-start.6 = (f32[6,256,256]{2,1,0:T(8,128)}, f32[6,256,256]{2,1,0:T(8,128)}, u32[]{:S(2)}, u32[]{:S(2)}) collective-permute-start(f32[6,256,256]{2,1,0:T(8,128)} %get-tuple-element.62), channel_id=1, source_target_pairs={{0,8},{9,17},{18,26},{27,3},{4,12},{13,21},{22,30},{31,7}} | collective-permute-start | bytes 4718600 | tf_op jit(solution)/shard_map/ppermute | solution.py:133
  403.7 2.9 copy-start.109
  447.0 4.1 copy-start.45
  448.1 2.0 copy-start.75
  480.2 3.4 copy-start.60
  484.3 19.5 %collective-permute-start.8 = (f32[6,256,256]{2,1,0:T(8,128)}, f32[6,256,256]{2,1,0:T(8,128)}, u32[]{:S(2)}, u32[]{:S(2)}) collective-permute-start(f32[6,256,256]{2,1,0:T(8,128)} %get-tuple-element.62), channel_id=1, source_target_pairs={{0,24},{9,1},{18,10},{27,19},{4,28},{13,5},{22,14},{31,23}} | collective-permute-start | bytes 4718600 | tf_op jit(solution)/shard_map/ppermute | solution.py:133
  492.1 5.1 copy-start.82
  492.1 11.7 %copy-start.2 = (f32[2,6,256,256]{3,2,1,0:T(8,128)S(1)}, f32[2,6,256,256]{3,2,1,0:T(8,128)}, u32[]{:S(2)}) copy-start(f32[2,6,256,256]{3,2,1,0:T(8,128)} %gather_fusion.1) | copy-start | bytes 9437188
  495.0 13.4 %slice-start = ((s8[4718592]{0:T(1024)(128)(4,1)}), s8[4194304]{0:T(1024)(128)(4,1)S(1)}, s32[]{:S(2)}) async-start(s8[4718592]{0:T(1024)(128)(4,1)} %bitcast.355), calls=%async_computation.3 | async-start | bytes 8388608
  497.6 10.8 %slice-start.1 = ((s8[4718592]{0:T(1024)(128)(4,1)}), s8[524288]{0:T(1024)(128)(4,1)S(1)}, s32[]{:S(2)}) async-start(s8[4718592]{0:T(1024)(128)(4,1)} %bitcast.355), calls=%async_computation.4 | async-start | bytes 1048576
  513.4 2.3 copy-start.38
  513.4 2.3 copy-start.68
  516.9 3.3 copy-start.21
  516.9 3.3 copy-start.44
  516.9 3.3 copy-start.74
  521.4 4.8 copy-start.46
  521.4 4.8 copy-start.76
  554.9 4.2 copy-start.4
  554.9 4.2 copy-start.7
  565.0 4.9 copy-start.1
  (67 other events, 84.3 us)
Sparse Core Ops, SparseCore 0:
  10.3 136.5 all-gather.4
  164.7 96.9 all-gather.6

commit v3 on v2

--- a/solution.py
+++ b/solution.py
@@ -46,11 +46,9 @@
     return lower, inverse
 
 
-def leading_factor(first, extra, row_count, col_count):
-    tile = first.shape[0]
-    grid = lax.all_gather(first, ("row", "col"), axis=0)
-    grid = grid.reshape(row_count, col_count, tile, tile)
-    pairs = [(i, j) for j in range(row_count, PANELS) for i in range(j, PANELS)]
+def leading_steps(grid, extra, lead, inverses, start, stop):
+    row_count, _, tile, _ = grid.shape
+
     def tile_at(i, j):
         if i < row_count:
             return grid[i, j]
@@ -58,10 +56,7 @@
             return grid[j, i].T
         return extra[i, j]
 
-    lead = {}
-    inverses = []
-    below = None
-    for k in range(PANELS):
+    for k in range(start, stop):
         column = jnp.concatenate([tile_at(i, k) for i in range(k, PANELS)], axis=0)
         if k:
             left = jnp.concatenate(
@@ -76,7 +71,6 @@
             below = dot_t(column[tile:], inverse)
             for i in range(k + 1, PANELS):
                 lead[i, k] = below[(i - k - 1) * tile:(i - k) * tile]
-    return lead, inverses
 
 
 def shards(parent_front, child_tiles, tile_target):
@@ -105,7 +99,15 @@
     present = jnp.any(sending, axis=1)
     picked = jnp.sum(jnp.where(sending, jnp.arange(stored, dtype=jnp.int32)[None, :], 0), axis=1)
     outgoing = jnp.where(present[:, None, None], held[picked], jnp.zeros((), jnp.bfloat16))
+    grid = lax.all_gather(front[0, :, 0, :], ("row", "col"), axis=0)
+    grid, outgoing = lax.optimization_barrier((grid, outgoing))
+    grid = grid.reshape(row_count, col_count, tile, tile)
     arrived = lax.all_to_all(outgoing, ("row", "col"), split_axis=0, concat_axis=0, tiled=True)
+    lead = {}
+    inverses = []
+    extra = {}
+    leading_steps(grid, extra, lead, inverses, 0, 2)
+    arrived, inverses[1] = lax.optimization_barrier((arrived, inverses[1]))
     landing = owner_all == myself
     came = jnp.any(landing, axis=1)
     where_to = jnp.sum(jnp.where(landing, local_all, 0), axis=1)
@@ -134,7 +136,6 @@
         parts.append(total)
     chosen = jnp.stack(parts, axis=1)
 
-    extra = {}
     if PANELS > row_count:
         corner = panel[row_count:, 0]
         holders = PANELS - row_count
@@ -148,7 +149,7 @@
                 full = jnp.where((my_row - r) % row_count == shift, received[shift], full)
             for j in range(r + 1):
                 extra[row_count + r, row_count + j] = full[j]
-    lead, inverses = leading_factor(front[0, :, 0, :], extra, row_count, col_count)
+    leading_steps(grid, extra, lead, inverses, 2, PANELS)
 
     stack = jnp.concatenate([panel, chosen], axis=1).reshape(PANELS, (count + lcols) * tile, tile)
     solved = []
@@ -171,10 +172,10 @@
     in_panel = (col_ids < PANELS)[None, None, :, None]
     below = jnp.where(in_panel, mine, trailing)
     zero = jnp.zeros((tile, tile), jnp.float32)
-    grid = jnp.stack([jnp.stack([lead.get((i, j), zero) for j in range(PANELS)]) for i in range(PANELS)])
+    factor = jnp.stack([jnp.stack([lead.get((i, j), zero) for j in range(PANELS)]) for i in range(PANELS)])
     tops = []
     for i in range(lead_rows):
-        picked_tile = grid[jnp.minimum(my_row + row_count * i, PANELS - 1), at]
+        picked_tile = factor[jnp.minimum(my_row + row_count * i, PANELS - 1), at]
         tops.append(jnp.where((col_ids < PANELS)[None, :, None], picked_tile[:, None, :], 0.0))
     out = []
     for i in range(lrows):

time: 586 us -> 617 us (1.053)
  waiting for transfers between devices: 133 us -> 169 us
    all_to_all x1, waiting for transfers between devices: 126 us -> 47.8 us  [shards(): lax.all_to_all(outgoing, ('row', 'col'), split_axis=0, concat_axis=0, til...]
    all_gather x1, waiting for transfers between devices: 0.02 us -> 62.7 us  [shards(): grid = lax.all_gather(front[0, :, 0, :], ('row', 'col'), axis=0)]
    all_gather x1, waiting for transfers between devices: 0.01 us -> 52.4 us  [shards(): panel = lax.all_gather(lower_front[:, 0], 'col', axis=0)[:PANELS]]
    all_gather x1 -> x0, local copies, waits for them, and re-layouts: 9.49 us -> none  [leading_factor(): grid = lax.all_gather(first, ('row', 'col'), axis=0)]
    optimization_barrier x0 -> x1, local copies, waits for them, and re-layouts: none -> 9.16 us  [shards(): grid, outgoing = lax.optimization_barrier((grid, outgoing))]
    unnamed x271 -> x268, local copies, waits for them, and re-layouts: 43.1 us -> 41.5 us
  transfers between devices with their start and end apart: 12 -> 12, of which waited for: 2 -> 4; matrix products, arithmetic and copies ran while one was open for 55% -> 34% of each run, Pallas kernels for 0% -> 0%
where the time goes in v3:
time: 617 us; the launch traced here: 610 us
  other arithmetic  197 us (32%)
  waiting for transfers between devices  169 us (27%)
  local copies, waits for them, and re-layouts  123 us (20%)
  matrix products  77.7 us (13%)
  starting transfers between devices  25.4 us (4%)
  between operations  17.9 us (3%)
    another operation x18, other arithmetic, tile_factor(): lax.linalg.cholesky(pivot[half:, half:] - dot_t(below, below), symmetrize...  77.6 us
    another operation x18, other arithmetic, tile_factor(): low1 = lax.linalg.cholesky(pivot[:half, :half], symmetrize_input=False)  76.6 us
    all_gather x1, waiting for transfers between devices, shards(): grid = lax.all_gather(front[0, :, 0, :], ('row', 'col'), axis=0)  62.7 us
    all_gather x1, waiting for transfers between devices, shards(): panel = lax.all_gather(lower_front[:, 0], 'col', axis=0)[:PANELS]  52.4 us
    dot_general x34, matrix products, dot_t(): return lax.dot_general(a, b, (((1,), (1,)), ((), ())), precision=HIGH)  47.8 us
    all_to_all x1, waiting for transfers between devices, shards(): lax.all_to_all(outgoing, ('row', 'col'), split_axis=0, concat_axis=0, til...  47.8 us
    unnamed x268, local copies, waits for them, and re-layouts  41.5 us
    dot_general x96, matrix products, dot(): return jnp.dot(a, b, precision=HIGH)  25 us
  transfers between devices with their start and end apart: 12, of which 4 were waited for; matrix products, arithmetic and copies ran while one was open for 34% of the time, Pallas kernels for 0%

profile of v3, /device:TPU:0, one launch (start us, length us, event | category | flops | bytes accessed | tf_op | source)
XLA Modules:
  0.0 610.1 jit_solution(2751905322576824522)
XLA Ops:
  6.5 1.9 copy.313
  9.3 3.7 slice.755
  13.7 3.8 copy.312
  19.2 2.8 gather_fusion
  23.3 4.5 broadcast_select_fusion
  27.8 62.7 %all-gather.5.cloned.1.call-done = f32[32,256,1,256]{3,1,2,0:T(8,128)} async-done(((f32[1,256,1,256]{3,1,2,0:T(8,128)}), f32[32,256,1,256]{3,1,2,0:T(8,128)}) %all-gather.5.cloned.1.call-update) | async-done | bytes 8388624 | tf_op jit(solution)/shard_map/all_gather | solution.py:102
  90.5 1.9 slice_bitcast_fusion.11
  93.4 9.2 %copy.192 = f32[32,256,256]{1,2,0:T(8,128)} copy(f32[32,256,256]{2,1,0:T(8,128)} %bitcast.367) | data formatting | bytes 16777216 | tf_op jit(solution)/shard_map/optimization_barrier | solution.py:103
  102.6 2.4 slice_bitcast_fusion.7
  105.1 11.7 %custom-call.14 = f32[128,128]{1,0:T(8,128)S(1)} custom-call(f32[128,128]{1,0:T(8,128)S(1)} %copy.193), custom_call_target="Cholesky" | custom-call | tf_op jit(solution)/shard_map/cholesky/custom-call.1 | solution.py:37
  120.3 11.7 %custom-call.15 = f32[128,128]{1,0:T(8,128)S(1)} custom-call(f32[128,128]{1,0:T(8,128)S(1)} %copy.195), custom_call_target="Cholesky" | custom-call | tf_op jit(solution)/shard_map/cholesky/custom-call.1 | solution.py:40
  142.1 1.6 convolution_subtract_fusion
  143.8 11.7 %custom-call.16 = f32[128,128]{1,0:T(8,128)S(1)} custom-call(f32[128,128]{1,0:T(8,128)S(1)} %slice.866), custom_call_target="Cholesky" | custom-call | tf_op jit(solution)/shard_map/cholesky/custom-call.1 | solution.py:37
  159.2 11.7 %custom-call.17 = f32[128,128]{1,0:T(8,128)S(1)} custom-call(f32[128,128]{1,0:T(8,128)S(1)} %convolution_subtract_fusion.4), custom_call_target="Cholesky" | custom-call | tf_op jit(solution)/shard_map/cholesky/custom-call.1 | solution.py:40
  183.8 11.7 %custom-call.18 = f32[128,128]{1,0:T(8,128)S(1)} custom-call(f32[128,128]{1,0:T(8,128)S(1)} %slice.902), custom_call_target="Cholesky" | custom-call | tf_op jit(solution)/shard_map/cholesky/custom-call.1 | solution.py:37
  198.4 3.7 all-to-all-start
  210.4 11.7 %custom-call.19 = f32[128,128]{1,0:T(8,128)S(1)} custom-call(f32[128,128]{1,0:T(8,128)S(1)} %convolution_subtract_fusion.3), custom_call_target="Cholesky" | custom-call | tf_op jit(solution)/shard_map/cholesky/custom-call.1 | solution.py:40
  225.9 1.8 fusion.100
  230.6 13.2 %custom-call.20 = f32[128,128]{1,0:T(8,128)} custom-call(f32[128,128]{1,0:T(8,128)} %slice.932), custom_call_target="Cholesky" | custom-call | tf_op jit(solution)/shard_map/cholesky/custom-call.1 | solution.py:37
  245.3 1.6 select_maximum_fusion.9
  246.9 2.1 fusion.443
  249.4 47.8 %all-to-all-done = bf16[32,256,256]{2,1,0:T(8,128)(2,1)} async-done(((bf16[32,256,256]{2,1,0:T(8,128)(2,1)}), bf16[32,256,256]{2,1,0:T(8,128)(2,1)}, u32[]{:S(2)}, u32[]{:S(2)}) %all-to-all-start) | async-done | bytes 4194336 | tf_op jit(solution)/shard_map/all_to_all | solution.py:105
  297.3 4.9 fusion.8
  309.3 1.7 fusion.411
  312.6 1.8 convolution_subtract_fusion.2
  314.4 13.2 %custom-call.21 = f32[128,128]{1,0:T(8,128)} custom-call(f32[128,128]{1,0:T(8,128)} %convolution_subtract_fusion.2), custom_call_target="Cholesky" | custom-call | tf_op jit(solution)/shard_map/cholesky/custom-call.1 | solution.py:40
  337.7 1.7 bitcast_dynamic-update-slice_fusion.8
  349.5 52.4 %all-gather.7.cloned.1.call-done = f32[24,1,256,256]{3,2,1,0:T(8,128)} async-done(((f32[3,1,256,256]{3,2,1,0:T(8,128)}), f32[24,1,256,256]{3,2,1,0:T(8,128)}) %all-gather.7.cloned.1.call-update) | async-done | bytes 6291472 | tf_op jit(solution)/shard_map/all_gather | solution.py:121
  401.8 1.9 slice_bitcast_fusion.2
  403.7 2.1 collective-permute-start.2
  405.8 3.4 collective-permute-start.1
  409.2 1.9 collective-permute-start
  411.9 4.9 slice.1005
  416.8 4.7 gather_fusion.1
  421.6 3.8 slice_bitcast_fusion.1
  425.4 1.9 collective-permute-start.4
  427.2 1.8 collective-permute-start.3
  429.0 1.8 collective-permute-start.5
  430.8 2.5 collective-permute-start.7
  433.3 3.9 collective-permute-start.6
  442.2 11.7 %custom-call.22 = f32[128,128]{1,0:T(8,128)S(1)} custom-call(f32[128,128]{1,0:T(8,128)S(1)} %slice.967), custom_call_target="Cholesky" | custom-call | tf_op jit(solution)/shard_map/cholesky/custom-call.1 | solution.py:37
  459.4 1.7 convolution_subtract_fusion.1
  461.1 12.5 %custom-call.23 = f32[128,128]{1,0:T(8,128)S(1)} custom-call(f32[128,128]{1,0:T(8,128)} %convolution_subtract_fusion.1), custom_call_target="Cholesky" | custom-call | tf_op jit(solution)/shard_map/cholesky/custom-call.1 | solution.py:40
  481.4 2.0 constant_dynamic-update-slice_fusion
  485.2 11.7 %custom-call.24 = f32[128,128]{1,0:T(8,128)S(1)} custom-call(f32[128,128]{1,0:T(8,128)S(1)} %slice.992), custom_call_target="Cholesky" | custom-call | tf_op jit(solution)/shard_map/cholesky/custom-call.1 | solution.py:37
  500.2 11.7 %custom-call.25 = f32[128,128]{1,0:T(8,128)S(1)} custom-call(f32[128,128]{1,0:T(8,128)S(1)} %slice_subtract_fusion), custom_call_target="Cholesky" | custom-call | tf_op jit(solution)/shard_map/cholesky/custom-call.1 | solution.py:40
  517.6 2.4 collective-permute-start.8
  522.5 2.8 bitcast_dynamic-update-slice_fusion.1
  525.3 2.9 bitcast_dynamic-update-slice_fusion
  528.3 1.9 dynamic-slice_bitcast_fusion.1
  530.9 6.2 %collective-permute-done.8 = f32[6,256,256]{2,1,0:T(8,128)} collective-permute-done((f32[6,256,256]{2,1,0:T(8,128)}, f32[6,256,256]{2,1,0:T(8,128)}, u32[]{:S(2)}, u32[]{:S(2)}) %collective-permute-start.8) | collective-permute-done | bytes 1572896 | tf_op jit(solution)/shard_map/ppermute | solution.py:135
  537.1 4.6 add_bitcast_fusion.1
  546.9 2.3 bitcast_subtract_fusion.3
  550.3 3.3 bitcast_subtract_fusion.2
  554.8 4.5 bitcast_subtract_fusion.1
  560.1 5.4 bitcast_subtract_fusion
  566.3 4.2 fusion.17
  570.5 2.5 slice.1024
  573.0 6.0 copy.252
  579.0 2.2 reshape.195
  581.2 6.9 %reshape.194 = f32[3,256,6,256]{3,2,1,0:T(8,128)} reshape(f32[768,1536]{1,0:T(8,128)} %copy.252) | data formatting | bytes 9437184 | tf_op jit(solution)/shard_map/reshape | solution.py:170
  588.1 3.7 constant_dynamic-slice_fusion
  592.3 3.9 fusion.43
  599.6 3.5 copy.255
  (566 shorter events, 126.5 us)
Async XLA Ops:
  6.5 12.7 %copy-start = (bf16[1,16,256,256]{3,2,1,0:T(8,128)(2,1)S(1)}, bf16[1,16,256,256]{3,2,1,0:T(8,128)(2,1)}, u32[]{:S(2)}) copy-start(bf16[1,16,256,256]{3,2,1,0:T(8,128)(2,1)} %param.5) | copy-start | bytes 6291460
  6.5 84.0 %all-gather.5.cloned.1.call-start = ((), (), s32[]{:S(2)}) async-start(), calls=%async_computation.1 | async-start | bytes 8650752 | tf_op jit(solution)/shard_map/all_gather | solution.py:102
  13.7 5.1 copy-start.112
  133.4 5.9 copy-start.21
  140.6 3.2 copy-start.34
  140.8 3.0 copy-start.67
  158.4 16.8 %copy-start.19 = (f32[128,128]{1,0:T(8,128)}, f32[128,128]{1,0:T(8,128)S(1)}, u32[]{:S(2)}) copy-start(f32[128,128]{1,0:T(8,128)S(1)} %fusion.86) | copy-start | bytes 196612
  175.0 3.7 copy-start.47
  175.2 3.5 copy-start.73
  175.3 3.6 copy-start.46
  176.9 2.8 copy-start.45
  178.8 2.6 copy-start.11
  179.8 3.0 copy-start.8
  196.9 9.5 %copy-start.24 = (f32[128,128]{1,0:T(8,128)}, f32[128,128]{1,0:T(8,128)S(1)}, u32[]{:S(2)}) copy-start(f32[128,128]{1,0:T(8,128)S(1)} %get-tuple-element.29) | copy-start | bytes 196612
  198.4 6.4 %copy-start.42 = (f32[256,256]{0,1:T(8,128)S(1)}, f32[256,256]{0,1:T(8,128)}, u32[]{:S(2)}) copy-start(f32[256,256]{0,1:T(8,128)} %get-tuple-element.43) | copy-start | bytes 786436
  198.4 7.2 %copy-start.44 = (f32[256,256]{0,1:T(8,128)S(1)}, f32[256,256]{0,1:T(8,128)}, u32[]{:S(2)}) copy-start(f32[256,256]{0,1:T(8,128)} %get-tuple-element.69) | copy-start | bytes 786436
  198.4 98.9 %all-to-all-start = ((bf16[32,256,256]{2,1,0:T(8,128)(2,1)}), bf16[32,256,256]{2,1,0:T(8,128)(2,1)}, u32[]{:S(2)}, u32[]{:S(2)}) async-start(bf16[32,256,256]{2,1,0:T(8,128)(2,1)} %broadcast_select_fusion), calls=%async_computation | async-start | bytes 8388608 | tf_op jit(solution)/shard_map/all_to_all | solution.py:105
  202.1 199.7 %all-gather.7.cloned.1.call-start = ((), (), s32[]{:S(2)}) async-start(), calls=%async_computation.2 | async-start | bytes 7077888 | tf_op jit(solution)/shard_map/all_gather | solution.py:121
  225.6 2.1 copy-start.32
  225.8 2.0 copy-start.12
  225.8 2.0 copy-start.49
  225.8 2.0 copy-start.54
  225.8 2.0 copy-start.83
  225.9 2.0 copy-start.87
  225.9 2.0 copy-start.97
  225.9 2.0 copy-start.99
  225.9 2.0 copy-start.100
  225.9 2.0 copy-start.108
  297.2 4.9 copy-start.7
  335.7 3.7 copy-start.9
  335.7 3.7 copy-start.55
  335.7 3.8 copy-start.50
  335.7 4.5 copy-start.5
  342.8 2.8 copy-start.36
  343.0 2.6 copy-start.69
  343.4 2.2 copy-start.43
  403.7 25.4 %collective-permute-start.2 = (f32[2,256,256]{2,1,0:T(8,128)}, f32[2,256,256]{2,1,0:T(8,128)}, u32[]{:S(2)}, u32[]{:S(2)}) collective-permute-start(f32[2,256,256]{2,1,0:T(8,128)} %slice_bitcast_fusion.2), channel_id=1, source_target_pairs={{0,8},{8,16},{1,9},{9,17},{2,10},{10,18},{3,11},{11,19},{4,12},{12... | collective-permute-start | bytes 1572872 | tf_op jit(solution)/shard_map/ppermute | solution.py:143
  405.8 25.1 %collective-permute-start.1 = (f32[2,256,256]{2,1,0:T(8,128)}, f32[2,256,256]{2,1,0:T(8,128)}, u32[]{:S(2)}, u32[]{:S(2)}) collective-permute-start(f32[2,256,256]{2,1,0:T(8,128)} %slice_bitcast_fusion.2), channel_id=1, source_target_pairs={{0,16},{8,24},{1,17},{9,25},{2,18},{10,26},{3,19},{11,27},{4,20},{... | collective-permute-start | bytes 1572872 | tf_op jit(solution)/shard_map/ppermute | solution.py:143
  409.2 24.1 %collective-permute-start = (f32[2,256,256]{2,1,0:T(8,128)}, f32[2,256,256]{2,1,0:T(8,128)}, u32[]{:S(2)}, u32[]{:S(2)}) collective-permute-start(f32[2,256,256]{2,1,0:T(8,128)} %slice_bitcast_fusion.2), channel_id=1, source_target_pairs={{0,24},{8,0},{1,25},{9,1},{2,26},{10,2},{3,27},{11,3},{4,28},{12,4... | collective-permute-start | bytes 1572872 | tf_op jit(solution)/shard_map/ppermute | solution.py:143
  425.4 92.2 %collective-permute-start.4 = (f32[6,256,256]{2,1,0:T(8,128)}, f32[6,256,256]{2,1,0:T(8,128)}, u32[]{:S(2)}, u32[]{:S(2)}) collective-permute-start(f32[6,256,256]{2,1,0:T(8,128)} %get-tuple-element.67), channel_id=1, source_target_pairs={{22,6},{31,15}} | collective-permute-start | bytes 4718600 | tf_op jit(solution)/shard_map/ppermute | solution.py:135
  427.2 103.6 %collective-permute-start.3 = (f32[6,256,256]{2,1,0:T(8,128)}, f32[6,256,256]{2,1,0:T(8,128)}, u32[]{:S(2)}, u32[]{:S(2)}) collective-permute-start(f32[6,256,256]{2,1,0:T(8,128)} %get-tuple-element.67), channel_id=1, source_target_pairs={{22,30},{31,7}} | collective-permute-start | bytes 4718600 | tf_op jit(solution)/shard_map/ppermute | solution.py:135
  429.0 101.8 %collective-permute-start.5 = (f32[6,256,256]{2,1,0:T(8,128)}, f32[6,256,256]{2,1,0:T(8,128)}, u32[]{:S(2)}, u32[]{:S(2)}) collective-permute-start(f32[6,256,256]{2,1,0:T(8,128)} %get-tuple-element.67), channel_id=1, source_target_pairs={{22,14},{31,23}} | collective-permute-start | bytes 4718600 | tf_op jit(solution)/shard_map/ppermute | solution.py:135
  430.8 100.0 %collective-permute-start.7 = (f32[6,256,256]{2,1,0:T(8,128)}, f32[6,256,256]{2,1,0:T(8,128)}, u32[]{:S(2)}, u32[]{:S(2)}) collective-permute-start(f32[6,256,256]{2,1,0:T(8,128)} %get-tuple-element.68), channel_id=1, source_target_pairs={{0,16},{9,25},{18,2},{27,11},{4,20},{13,29},{22,6},{31,15}} | collective-permute-start | bytes 4718600 | tf_op jit(solution)/shard_map/ppermute | solution.py:135
  433.3 97.6 %collective-permute-start.6 = (f32[6,256,256]{2,1,0:T(8,128)}, f32[6,256,256]{2,1,0:T(8,128)}, u32[]{:S(2)}, u32[]{:S(2)}) collective-permute-start(f32[6,256,256]{2,1,0:T(8,128)} %get-tuple-element.68), channel_id=1, source_target_pairs={{0,8},{9,17},{18,26},{27,3},{4,12},{13,21},{22,30},{31,7}} | collective-permute-start | bytes 4718600 | tf_op jit(solution)/shard_map/ppermute | solution.py:135
  437.2 2.9 copy-start.105
  480.4 4.1 copy-start.38
  481.4 2.0 copy-start.71
  513.4 3.4 copy-start.57
  517.6 19.5 %collective-permute-start.8 = (f32[6,256,256]{2,1,0:T(8,128)}, f32[6,256,256]{2,1,0:T(8,128)}, u32[]{:S(2)}, u32[]{:S(2)}) collective-permute-start(f32[6,256,256]{2,1,0:T(8,128)} %get-tuple-element.68), channel_id=1, source_target_pairs={{0,24},{9,1},{18,10},{27,19},{4,28},{13,5},{22,14},{31,23}} | collective-permute-start | bytes 4718600 | tf_op jit(solution)/shard_map/ppermute | solution.py:135
  525.3 5.1 copy-start.79
  525.3 11.8 %copy-start.2 = (f32[2,6,256,256]{3,2,1,0:T(8,128)S(1)}, f32[2,6,256,256]{3,2,1,0:T(8,128)}, u32[]{:S(2)}) copy-start(f32[2,6,256,256]{3,2,1,0:T(8,128)} %gather_fusion.1) | copy-start | bytes 9437188
  528.3 13.4 %slice-start = ((s8[4718592]{0:T(1024)(128)(4,1)}), s8[4194304]{0:T(1024)(128)(4,1)S(1)}, s32[]{:S(2)}) async-start(s8[4718592]{0:T(1024)(128)(4,1)} %bitcast.356), calls=%async_computation.3 | async-start | bytes 8388608
  530.8 10.9 %slice-start.1 = ((s8[4718592]{0:T(1024)(128)(4,1)}), s8[524288]{0:T(1024)(128)(4,1)S(1)}, s32[]{:S(2)}) async-start(s8[4718592]{0:T(1024)(128)(4,1)} %bitcast.356), calls=%async_computation.4 | async-start | bytes 1048576
  546.9 2.3 copy-start.33
  546.9 2.3 copy-start.66
  550.3 3.3 copy-start.18
  550.3 3.3 copy-start.37
  550.3 3.3 copy-start.70
  554.8 4.5 copy-start.39
  554.8 4.5 copy-start.72
  588.1 4.2 copy-start.3
  588.1 4.2 copy-start.6
  588.1 4.3 copy-start.114
  598.2 4.9 copy-start.1
  (65 other events, 82.6 us)
Sparse Core Ops, SparseCore 0:
  10.3 80.1 all-gather.4
  304.6 97.1 all-gather.6
